TPU v7x, 256 devices: a whole 4x4x8 slice. The times are simulated.
256 devices in a mesh: feeder: 16 (over z, core), tm: 16 (over y, x).
Axes of the slice: x: 4, y: 4, z: 8, core: 2. Of those that a mesh axis runs over, the one named last changes fastest.
Arguments:
- node_load: bfloat16 [256, 64, 96, 512], P('feeder', None, 'tm'), may hold values from -6 to 6
- drive_map: bfloat16 [256, 512, 256], P('feeder'), may hold values from -0.25 to 0.25
- decay_rate: float32 [256, 96, 256], P('feeder', 'tm'), may hold values from 0.45 to 1
- counts: int32 [256], P('feeder'), may hold values from 64 to 256
- out_map: float32 [256, 2, 256], P('feeder'), may hold values from -0.375 to 0.375
- area_of: int32 [256, 1], replicated, may hold values from 0 to 15; in each aligned block of 16 rows (0 to 15, 16 to 31, ...) at most 2 rows name the same one
- head_bus: int32 [256], replicated, may hold values from 0 to 255
- rule_of: int32 [256], replicated, may hold values from 0 to 15
- rule_knots: int32 [16, 8], replicated, may hold values from -3200 to 2400, as said below
- levels: int32 [16, 8], replicated, may hold values from -1000 to 1000
- sensitivity: float32 [16, 2, 256, 256], P('feeder'), may hold values from -0.6 to 0.6
Outputs:
- setpoints: float32 [256, 96, 64], P('feeder', 'tm')
Inputs may be any that keep to these rules, and one draw needn't show every extreme that they name: `area_of`: in each aligned block of 16 feeders no area is named by more than 2 feeders, a bound that some block reaches. `rule_knots`: each row strictly increasing, neighbouring breakpoints 200 to 800 apart.
All inputs are finite; a program needn't handle non-finite values.
Results may differ from a plain program's by a relative error of at most 0.00045.
Values sent between devices are 32-bit elements; how exact they have to be, the bound alone decides.
No kernel may reach another device: no remote copies, remote signals or barrier semaphores. Data moves between devices by JAX's collectives and lax.ppermute only.
A program may use at most 64 MiB of HBM per device.

v0:
```python
import jax
import jax.numpy as jnp
from jax import lax
from jax.sharding import PartitionSpec as P


def passed_along(block, axis, distance):
    devices = range(lax.axis_size(axis))
    route = [(i - distance, i) for i in devices if i - distance in devices]
    return lax.ppermute(block, axis, route)


def setpoint_rule(volts, knot_volts, knot_levels):
    result = knot_levels[..., 0:1] + jnp.zeros_like(volts)
    for piece in range(knot_volts.shape[-1] - 1):
        span_width = knot_volts[..., piece + 1 : piece + 2] - knot_volts[..., piece : piece + 1]
        slope = (
            knot_levels[..., piece + 1 : piece + 2] - knot_levels[..., piece : piece + 1]
        ) / span_width
        result = result + slope * jnp.clip(
            volts - knot_volts[..., piece : piece + 1], 0.0, span_width
        )
    return result


def per_device(
    node_load,
    drive_map,
    decay_rate,
    counts,
    out_map,
    area_of,
    head_bus,
    rule_of,
    rule_knots,
    levels,
    sensitivity,
):
    per_dev, scenarios, span_len, node_count = node_load.shape
    state_width = drive_map.shape[2]
    bus_count = sensitivity.shape[2]
    state_ids = jnp.arange(state_width, dtype=jnp.int32)
    live = (state_ids[None, :] < counts[:, None]).astype(jnp.float32)
    drive = (
        jnp.einsum("fctn,fns->fcts", node_load, drive_map, preferred_element_type=jnp.float32)
        * live[:, None, None, :]
    )
    local_state = jnp.zeros((per_dev, scenarios, state_width), jnp.float32)
    decay_prod = jnp.ones((per_dev, state_width), jnp.float32)
    history_record = []
    products = []
    for moment in range(span_len):
        retain = decay_rate[:, moment, :]
        local_state = retain[:, None, :] * local_state + drive[:, :, moment, :]
        decay_prod = decay_prod * retain
        history_record.append(local_state)
        products.append(decay_prod)

    def one_turn(turn_index, incoming):
        return passed_along(local_state + decay_prod[:, None, :] * incoming, "tm", 1)

    incoming = lax.fori_loop(0, lax.axis_size("tm") - 1, one_turn, jnp.zeros_like(local_state))
    states = (
        jnp.stack(history_record, 2)
        + jnp.stack(products, 1)[:, None, :, :] * incoming[:, :, None, :]
    )
    head_flow = jnp.einsum("fcts,fks->fktc", states, out_map, precision=lax.Precision.HIGHEST)
    head_flow = head_flow.reshape(per_dev, 2, span_len * scenarios)
    area_ids = area_of[:, 0]
    owner = lax.axis_index("feeder")
    rule_count = rule_knots.shape[0]
    rule_hot = (rule_of[:, None] == jnp.arange(rule_count, dtype=jnp.int32)[None, :]).astype(
        jnp.float32
    )
    knot_volts = (
        jnp.dot(rule_hot, rule_knots.astype(jnp.float32), precision=lax.Precision.HIGHEST) / 1000.0
    )
    knot_levels = (
        jnp.dot(rule_hot, levels.astype(jnp.float32), precision=lax.Precision.HIGHEST) / 1000.0
    )
    bus_ids = jnp.arange(bus_count, dtype=jnp.int32)
    area_sens = sensitivity[0]
    every_flow = lax.all_gather(head_flow, "feeder", axis=0, tiled=True)
    mine = (area_ids == owner).astype(jnp.float32)
    chosen = (head_bus[:, None] == bus_ids[None, :]).astype(jnp.float32) * mine[:, None]
    bus_flow = jnp.einsum("fb,fkr->kbr", chosen, every_flow, precision=lax.Precision.HIGHEST)
    volt_shift = jnp.einsum("kbe,ker->br", area_sens, bus_flow, precision=lax.Precision.HIGHEST)
    volts = jnp.einsum("fb,br->fr", chosen, volt_shift, precision=lax.Precision.HIGHEST)
    settings = setpoint_rule(volts, knot_volts, knot_levels) * mine[:, None]
    mine_back = lax.psum_scatter(settings, "feeder", scatter_dimension=0, tiled=True)
    return mine_back.reshape(per_dev, span_len, scenarios)


def solution(mesh):
    return jax.shard_map(
        per_device,
        mesh=mesh,
        in_specs=(
            P("feeder", None, "tm", None),
            P("feeder", None, None),
            P("feeder", "tm", None),
            P("feeder"),
            P("feeder", None, None),
            P(),
            P(),
            P(),
            P(),
            P(),
            P("feeder", None, None, None),
        ),
        out_specs=P("feeder", "tm", None),
        check_vma=False,
    )
```

profile of v0, /device:TPU:1, one launch (start us, length us, event | category | flops | bytes accessed | tf_op | source)
XLA Modules:
  0.0 510.4 jit_solution(4740443761466845442)
XLA Ops:
  14.6 5.8 %broadcast_multiply_fusion = f32[16,64,6,256]{3,1,2,0:T(8,128)S(1)} fusion(f32[16,256]{1,0:T(8,128)S(1)} %fusion.37, bf16[16,64,6,512]{3,1,2,0:T(8,128)(2,1)} %param.13, bf16[16,512,256]{2,1,0:T(8,128)(2,1)} %param.14), kind=kOutput, calls=%fused_computation.6 | convolution fusion | flops 1612185600 | bytes 16793600 | tf_op jit(solution)/shard_map/fctn,fns->fcts/dot_general | solution.py:45
  28.4 354.2 %while.10 = (s32[]{:T(128)}, f32[16,64,256]{2,1,0:T(8,128)S(1)}, f32[16,256]{1,0:T(8,128)S(1)}, f32[16,64,256]{2,1,0:T(8,128)S(1)}, s32[]{:T(128)}) while((s32[]{:T(128)}, f32[16,64,256]{2,1,0:T(8,128)S(1)}, f32[16,256]{1,0:T(8,128)S(1)}, f32[16,64,256]{2,1,0:T(8,128)S(1)}, s32[]{:T(128)}) %tuple.52), condition=%wide.region_1.0_spmd, body=%wide.region_0.0_spmd.sunk | while | flops 524290 | bytes 7356517 | solution.py:62
  33.6 22.1 %collective-permute-done = f32[16,64,256]{2,1,0:T(8,128)S(1)} collective-permute-done((f32[16,64,256]{2,1,0:T(8,128)}, f32[16,64,256]{2,1,0:T(8,128)S(1)}, u32[]{:S(2)}, u32[]{:S(2)}) %collective-permute-start) | collective-permute-done | bytes 1048608 | tf_op jit(solution)/shard_map/while/body/eval_jaxpr/ppermute | solution.py:10
  56.9 4.1 collective-permute-start
  60.9 21.1 %collective-permute-done = f32[16,64,256]{2,1,0:T(8,128)S(1)} collective-permute-done((f32[16,64,256]{2,1,0:T(8,128)}, f32[16,64,256]{2,1,0:T(8,128)S(1)}, u32[]{:S(2)}, u32[]{:S(2)}) %collective-permute-start) | collective-permute-done | bytes 1048608 | tf_op jit(solution)/shard_map/while/body/eval_jaxpr/ppermute | solution.py:10
  83.3 4.1 collective-permute-start
  87.3 20.2 %collective-permute-done = f32[16,64,256]{2,1,0:T(8,128)S(1)} collective-permute-done((f32[16,64,256]{2,1,0:T(8,128)}, f32[16,64,256]{2,1,0:T(8,128)S(1)}, u32[]{:S(2)}, u32[]{:S(2)}) %collective-permute-start) | collective-permute-done | bytes 1048608 | tf_op jit(solution)/shard_map/while/body/eval_jaxpr/ppermute | solution.py:10
  112.8 19.3 %collective-permute-done = f32[16,64,256]{2,1,0:T(8,128)S(1)} collective-permute-done((f32[16,64,256]{2,1,0:T(8,128)}, f32[16,64,256]{2,1,0:T(8,128)S(1)}, u32[]{:S(2)}, u32[]{:S(2)}) %collective-permute-start) | collective-permute-done | bytes 1048608 | tf_op jit(solution)/shard_map/while/body/eval_jaxpr/ppermute | solution.py:10
  137.3 18.4 %collective-permute-done = f32[16,64,256]{2,1,0:T(8,128)S(1)} collective-permute-done((f32[16,64,256]{2,1,0:T(8,128)}, f32[16,64,256]{2,1,0:T(8,128)S(1)}, u32[]{:S(2)}, u32[]{:S(2)}) %collective-permute-start) | collective-permute-done | bytes 1048608 | tf_op jit(solution)/shard_map/while/body/eval_jaxpr/ppermute | solution.py:10
  156.8 5.3 %collective-permute-start = (f32[16,64,256]{2,1,0:T(8,128)}, f32[16,64,256]{2,1,0:T(8,128)S(1)}, u32[]{:S(2)}, u32[]{:S(2)}) collective-permute-start(f32[16,64,256]{2,1,0:T(8,128)} %multiply_add_fusion.5), channel_id=1, source_target_pairs={{0,1},{1,2},{2,3},{3,4},{4,5},{5,6},{6,7},{7,8},{8,9},{9,10},{10,1... | collective-permute-start | bytes 3145736 | tf_op jit(solution)/shard_map/while/body/eval_jaxpr/ppermute | solution.py:10
  162.2 17.4 %collective-permute-done = f32[16,64,256]{2,1,0:T(8,128)S(1)} collective-permute-done((f32[16,64,256]{2,1,0:T(8,128)}, f32[16,64,256]{2,1,0:T(8,128)S(1)}, u32[]{:S(2)}, u32[]{:S(2)}) %collective-permute-start) | collective-permute-done | bytes 1048608 | tf_op jit(solution)/shard_map/while/body/eval_jaxpr/ppermute | solution.py:10
  180.8 6.2 %collective-permute-start = (f32[16,64,256]{2,1,0:T(8,128)}, f32[16,64,256]{2,1,0:T(8,128)S(1)}, u32[]{:S(2)}, u32[]{:S(2)}) collective-permute-start(f32[16,64,256]{2,1,0:T(8,128)} %multiply_add_fusion.5), channel_id=1, source_target_pairs={{0,1},{1,2},{2,3},{3,4},{4,5},{5,6},{6,7},{7,8},{8,9},{9,10},{10,1... | collective-permute-start | bytes 3145736 | tf_op jit(solution)/shard_map/while/body/eval_jaxpr/ppermute | solution.py:10
  187.0 16.5 %collective-permute-done = f32[16,64,256]{2,1,0:T(8,128)S(1)} collective-permute-done((f32[16,64,256]{2,1,0:T(8,128)}, f32[16,64,256]{2,1,0:T(8,128)S(1)}, u32[]{:S(2)}, u32[]{:S(2)}) %collective-permute-start) | collective-permute-done | bytes 1048608 | tf_op jit(solution)/shard_map/while/body/eval_jaxpr/ppermute | solution.py:10
  204.7 6.2 %collective-permute-start = (f32[16,64,256]{2,1,0:T(8,128)}, f32[16,64,256]{2,1,0:T(8,128)S(1)}, u32[]{:S(2)}, u32[]{:S(2)}) collective-permute-start(f32[16,64,256]{2,1,0:T(8,128)} %multiply_add_fusion.5), channel_id=1, source_target_pairs={{0,1},{1,2},{2,3},{3,4},{4,5},{5,6},{6,7},{7,8},{8,9},{9,10},{10,1... | collective-permute-start | bytes 3145736 | tf_op jit(solution)/shard_map/while/body/eval_jaxpr/ppermute | solution.py:10
  210.9 15.6 %collective-permute-done = f32[16,64,256]{2,1,0:T(8,128)S(1)} collective-permute-done((f32[16,64,256]{2,1,0:T(8,128)}, f32[16,64,256]{2,1,0:T(8,128)S(1)}, u32[]{:S(2)}, u32[]{:S(2)}) %collective-permute-start) | collective-permute-done | bytes 1048608 | tf_op jit(solution)/shard_map/while/body/eval_jaxpr/ppermute | solution.py:10
  227.6 6.2 %collective-permute-start = (f32[16,64,256]{2,1,0:T(8,128)}, f32[16,64,256]{2,1,0:T(8,128)S(1)}, u32[]{:S(2)}, u32[]{:S(2)}) collective-permute-start(f32[16,64,256]{2,1,0:T(8,128)} %multiply_add_fusion.5), channel_id=1, source_target_pairs={{0,1},{1,2},{2,3},{3,4},{4,5},{5,6},{6,7},{7,8},{8,9},{9,10},{10,1... | collective-permute-start | bytes 3145736 | tf_op jit(solution)/shard_map/while/body/eval_jaxpr/ppermute | solution.py:10
  233.8 14.7 %collective-permute-done = f32[16,64,256]{2,1,0:T(8,128)S(1)} collective-permute-done((f32[16,64,256]{2,1,0:T(8,128)}, f32[16,64,256]{2,1,0:T(8,128)S(1)}, u32[]{:S(2)}, u32[]{:S(2)}) %collective-permute-start) | collective-permute-done | bytes 1048608 | tf_op jit(solution)/shard_map/while/body/eval_jaxpr/ppermute | solution.py:10
  249.7 6.2 %collective-permute-start = (f32[16,64,256]{2,1,0:T(8,128)}, f32[16,64,256]{2,1,0:T(8,128)S(1)}, u32[]{:S(2)}, u32[]{:S(2)}) collective-permute-start(f32[16,64,256]{2,1,0:T(8,128)} %multiply_add_fusion.5), channel_id=1, source_target_pairs={{0,1},{1,2},{2,3},{3,4},{4,5},{5,6},{6,7},{7,8},{8,9},{9,10},{10,1... | collective-permute-start | bytes 3145736 | tf_op jit(solution)/shard_map/while/body/eval_jaxpr/ppermute | solution.py:10
  255.8 14.3 %collective-permute-done = f32[16,64,256]{2,1,0:T(8,128)S(1)} collective-permute-done((f32[16,64,256]{2,1,0:T(8,128)}, f32[16,64,256]{2,1,0:T(8,128)S(1)}, u32[]{:S(2)}, u32[]{:S(2)}) %collective-permute-start) | collective-permute-done | bytes 1048608 | tf_op jit(solution)/shard_map/while/body/eval_jaxpr/ppermute | solution.py:10
  271.3 6.2 %collective-permute-start = (f32[16,64,256]{2,1,0:T(8,128)}, f32[16,64,256]{2,1,0:T(8,128)S(1)}, u32[]{:S(2)}, u32[]{:S(2)}) collective-permute-start(f32[16,64,256]{2,1,0:T(8,128)} %multiply_add_fusion.5), channel_id=1, source_target_pairs={{0,1},{1,2},{2,3},{3,4},{4,5},{5,6},{6,7},{7,8},{8,9},{9,10},{10,1... | collective-permute-start | bytes 3145736 | tf_op jit(solution)/shard_map/while/body/eval_jaxpr/ppermute | solution.py:10
  277.5 14.3 %collective-permute-done = f32[16,64,256]{2,1,0:T(8,128)S(1)} collective-permute-done((f32[16,64,256]{2,1,0:T(8,128)}, f32[16,64,256]{2,1,0:T(8,128)S(1)}, u32[]{:S(2)}, u32[]{:S(2)}) %collective-permute-start) | collective-permute-done | bytes 1048608 | tf_op jit(solution)/shard_map/while/body/eval_jaxpr/ppermute | solution.py:10
  292.9 6.2 %collective-permute-start = (f32[16,64,256]{2,1,0:T(8,128)}, f32[16,64,256]{2,1,0:T(8,128)S(1)}, u32[]{:S(2)}, u32[]{:S(2)}) collective-permute-start(f32[16,64,256]{2,1,0:T(8,128)} %multiply_add_fusion.5), channel_id=1, source_target_pairs={{0,1},{1,2},{2,3},{3,4},{4,5},{5,6},{6,7},{7,8},{8,9},{9,10},{10,1... | collective-permute-start | bytes 3145736 | tf_op jit(solution)/shard_map/while/body/eval_jaxpr/ppermute | solution.py:10
  299.1 14.3 %collective-permute-done = f32[16,64,256]{2,1,0:T(8,128)S(1)} collective-permute-done((f32[16,64,256]{2,1,0:T(8,128)}, f32[16,64,256]{2,1,0:T(8,128)S(1)}, u32[]{:S(2)}, u32[]{:S(2)}) %collective-permute-start) | collective-permute-done | bytes 1048608 | tf_op jit(solution)/shard_map/while/body/eval_jaxpr/ppermute | solution.py:10
  314.5 6.2 %collective-permute-start = (f32[16,64,256]{2,1,0:T(8,128)}, f32[16,64,256]{2,1,0:T(8,128)S(1)}, u32[]{:S(2)}, u32[]{:S(2)}) collective-permute-start(f32[16,64,256]{2,1,0:T(8,128)} %multiply_add_fusion.5), channel_id=1, source_target_pairs={{0,1},{1,2},{2,3},{3,4},{4,5},{5,6},{6,7},{7,8},{8,9},{9,10},{10,1... | collective-permute-start | bytes 3145736 | tf_op jit(solution)/shard_map/while/body/eval_jaxpr/ppermute | solution.py:10
  320.7 15.0 %collective-permute-done = f32[16,64,256]{2,1,0:T(8,128)S(1)} collective-permute-done((f32[16,64,256]{2,1,0:T(8,128)}, f32[16,64,256]{2,1,0:T(8,128)S(1)}, u32[]{:S(2)}, u32[]{:S(2)}) %collective-permute-start) | collective-permute-done | bytes 1048608 | tf_op jit(solution)/shard_map/while/body/eval_jaxpr/ppermute | solution.py:10
  336.8 6.2 %collective-permute-start = (f32[16,64,256]{2,1,0:T(8,128)}, f32[16,64,256]{2,1,0:T(8,128)S(1)}, u32[]{:S(2)}, u32[]{:S(2)}) collective-permute-start(f32[16,64,256]{2,1,0:T(8,128)} %multiply_add_fusion.5), channel_id=1, source_target_pairs={{0,1},{1,2},{2,3},{3,4},{4,5},{5,6},{6,7},{7,8},{8,9},{9,10},{10,1... | collective-permute-start | bytes 3145736 | tf_op jit(solution)/shard_map/while/body/eval_jaxpr/ppermute | solution.py:10
  343.0 15.7 %collective-permute-done = f32[16,64,256]{2,1,0:T(8,128)S(1)} collective-permute-done((f32[16,64,256]{2,1,0:T(8,128)}, f32[16,64,256]{2,1,0:T(8,128)S(1)}, u32[]{:S(2)}, u32[]{:S(2)}) %collective-permute-start) | collective-permute-done | bytes 1048608 | tf_op jit(solution)/shard_map/while/body/eval_jaxpr/ppermute | solution.py:10
  359.9 6.2 %collective-permute-start = (f32[16,64,256]{2,1,0:T(8,128)}, f32[16,64,256]{2,1,0:T(8,128)S(1)}, u32[]{:S(2)}, u32[]{:S(2)}) collective-permute-start(f32[16,64,256]{2,1,0:T(8,128)} %multiply_add_fusion.5), channel_id=1, source_target_pairs={{0,1},{1,2},{2,3},{3,4},{4,5},{5,6},{6,7},{7,8},{8,9},{9,10},{10,1... | collective-permute-start | bytes 3145736 | tf_op jit(solution)/shard_map/while/body/eval_jaxpr/ppermute | solution.py:10
  366.1 16.5 %collective-permute-done = f32[16,64,256]{2,1,0:T(8,128)S(1)} collective-permute-done((f32[16,64,256]{2,1,0:T(8,128)}, f32[16,64,256]{2,1,0:T(8,128)S(1)}, u32[]{:S(2)}, u32[]{:S(2)}) %collective-permute-start) | collective-permute-done | bytes 1048608 | tf_op jit(solution)/shard_map/while/body/eval_jaxpr/ppermute | solution.py:10
  382.7 16.8 %fusion.6 = f32[16,2,6,64]{3,1,2,0:T(2,128)S(1)} fusion(f32[16,2,256]{2,1,0:T(2,128)S(1)} %copy-done.1, f32[16,64,6,256]{3,1,0,2:T(8,128)} %fusion.15, f32[16,64,256]{2,1,0:T(8,128)S(1)} %get-tuple-element.27, f32[16,6,256]{2,0,1:T(8,128)S(1)} %get-tuple-element.56), kind=kOutput, calls=%fused_computation.9 | convolution fusion | flops 40894464 | bytes 7520256 | tf_op jit(solution)/shard_map/fcts,fks->fktc/dot_general | solution.py:67
  399.5 36.0 %all_gather.3 = f32[256,2,384]{2,0,1:T(8,128)S(1)} all-gather(f32[16,2,384]{2,0,1:T(8,128)S(1)} %reshape.29), channel_id=1, replica_groups=mesh['feeder'=16,'tm'=16] {'feeder'}, dimensions={0}, use_global_device_ids=true | all-gather | bytes 835584 | tf_op jit(solution)/shard_map/all_gather | solution.py:83
  440.1 62.0 %reduce-scatter.2.cloned.1.call-done = f32[16,384]{1,0:T(8,128)} async-done(((f32[256,384]{1,0:T(8,128)}), f32[16,384]{1,0:T(8,128)}) %reduce-scatter.2.cloned.1.call-update) | async-done | bytes 24592 | tf_op jit(solution)/shard_map/reduce_scatter | solution.py:90
  (56 shorter events, 51.9 us)
Async XLA Ops:
  6.5 430.5 %copy-start = (f32[1,2,256,256]{3,2,1,0:T(8,128)S(1)}, f32[1,2,256,256]{3,2,1,0:T(8,128)}, u32[]{:S(2)}) copy-start(f32[1,2,256,256]{3,2,1,0:T(8,128)} %param.23) | copy-start | bytes 1572868
  6.5 495.5 %reduce-scatter.2.cloned.1.call-start = ((), (), s32[]{:S(2)}) async-start(), calls=%async_computation.1 | async-start | bytes 417792 | tf_op jit(solution)/shard_map/reduce_scatter | solution.py:90
  28.4 354.2 %copy-start.1 = (f32[16,2,256]{2,1,0:T(2,128)S(1)}, f32[16,2,256]{2,1,0:T(2,128)}, u32[]{:S(2)}) copy-start(f32[16,2,256]{2,1,0:T(2,128)} %param.17) | copy-start | bytes 98308
  29.6 26.1 %collective-permute-start = (f32[16,64,256]{2,1,0:T(8,128)}, f32[16,64,256]{2,1,0:T(8,128)S(1)}, u32[]{:S(2)}, u32[]{:S(2)}) collective-permute-start(f32[16,64,256]{2,1,0:T(8,128)} %multiply_add_fusion.5), channel_id=1, source_target_pairs={{0,1},{1,2},{2,3},{3,4},{4,5},{5,6},{6,7},{7,8},{8,9},{9,10},{10,1... | collective-permute-start | bytes 3145736 | tf_op jit(solution)/shard_map/while/body/eval_jaxpr/ppermute | solution.py:10
  56.9 25.2 %collective-permute-start = (f32[16,64,256]{2,1,0:T(8,128)}, f32[16,64,256]{2,1,0:T(8,128)S(1)}, u32[]{:S(2)}, u32[]{:S(2)}) collective-permute-start(f32[16,64,256]{2,1,0:T(8,128)} %multiply_add_fusion.5), channel_id=1, source_target_pairs={{0,1},{1,2},{2,3},{3,4},{4,5},{5,6},{6,7},{7,8},{8,9},{9,10},{10,1... | collective-permute-start | bytes 3145736 | tf_op jit(solution)/shard_map/while/body/eval_jaxpr/ppermute | solution.py:10
  83.3 24.3 %collective-permute-start = (f32[16,64,256]{2,1,0:T(8,128)}, f32[16,64,256]{2,1,0:T(8,128)S(1)}, u32[]{:S(2)}, u32[]{:S(2)}) collective-permute-start(f32[16,64,256]{2,1,0:T(8,128)} %multiply_add_fusion.5), channel_id=1, source_target_pairs={{0,1},{1,2},{2,3},{3,4},{4,5},{5,6},{6,7},{7,8},{8,9},{9,10},{10,1... | collective-permute-start | bytes 3145736 | tf_op jit(solution)/shard_map/while/body/eval_jaxpr/ppermute | solution.py:10
  108.7 23.4 %collective-permute-start = (f32[16,64,256]{2,1,0:T(8,128)}, f32[16,64,256]{2,1,0:T(8,128)S(1)}, u32[]{:S(2)}, u32[]{:S(2)}) collective-permute-start(f32[16,64,256]{2,1,0:T(8,128)} %multiply_add_fusion.5), channel_id=1, source_target_pairs={{0,1},{1,2},{2,3},{3,4},{4,5},{5,6},{6,7},{7,8},{8,9},{9,10},{10,1... | collective-permute-start | bytes 3145736 | tf_op jit(solution)/shard_map/while/body/eval_jaxpr/ppermute | solution.py:10
  133.2 22.4 %collective-permute-start = (f32[16,64,256]{2,1,0:T(8,128)}, f32[16,64,256]{2,1,0:T(8,128)S(1)}, u32[]{:S(2)}, u32[]{:S(2)}) collective-permute-start(f32[16,64,256]{2,1,0:T(8,128)} %multiply_add_fusion.5), channel_id=1, source_target_pairs={{0,1},{1,2},{2,3},{3,4},{4,5},{5,6},{6,7},{7,8},{8,9},{9,10},{10,1... | collective-permute-start | bytes 3145736 | tf_op jit(solution)/shard_map/while/body/eval_jaxpr/ppermute | solution.py:10
  156.8 22.8 %collective-permute-start = (f32[16,64,256]{2,1,0:T(8,128)}, f32[16,64,256]{2,1,0:T(8,128)S(1)}, u32[]{:S(2)}, u32[]{:S(2)}) collective-permute-start(f32[16,64,256]{2,1,0:T(8,128)} %multiply_add_fusion.5), channel_id=1, source_target_pairs={{0,1},{1,2},{2,3},{3,4},{4,5},{5,6},{6,7},{7,8},{8,9},{9,10},{10,1... | collective-permute-start | bytes 3145736 | tf_op jit(solution)/shard_map/while/body/eval_jaxpr/ppermute | solution.py:10
  180.8 22.7 %collective-permute-start = (f32[16,64,256]{2,1,0:T(8,128)}, f32[16,64,256]{2,1,0:T(8,128)S(1)}, u32[]{:S(2)}, u32[]{:S(2)}) collective-permute-start(f32[16,64,256]{2,1,0:T(8,128)} %multiply_add_fusion.5), channel_id=1, source_target_pairs={{0,1},{1,2},{2,3},{3,4},{4,5},{5,6},{6,7},{7,8},{8,9},{9,10},{10,1... | collective-permute-start | bytes 3145736 | tf_op jit(solution)/shard_map/while/body/eval_jaxpr/ppermute | solution.py:10
  204.7 21.8 %collective-permute-start = (f32[16,64,256]{2,1,0:T(8,128)}, f32[16,64,256]{2,1,0:T(8,128)S(1)}, u32[]{:S(2)}, u32[]{:S(2)}) collective-permute-start(f32[16,64,256]{2,1,0:T(8,128)} %multiply_add_fusion.5), channel_id=1, source_target_pairs={{0,1},{1,2},{2,3},{3,4},{4,5},{5,6},{6,7},{7,8},{8,9},{9,10},{10,1... | collective-permute-start | bytes 3145736 | tf_op jit(solution)/shard_map/while/body/eval_jaxpr/ppermute | solution.py:10
  227.6 20.9 %collective-permute-start = (f32[16,64,256]{2,1,0:T(8,128)}, f32[16,64,256]{2,1,0:T(8,128)S(1)}, u32[]{:S(2)}, u32[]{:S(2)}) collective-permute-start(f32[16,64,256]{2,1,0:T(8,128)} %multiply_add_fusion.5), channel_id=1, source_target_pairs={{0,1},{1,2},{2,3},{3,4},{4,5},{5,6},{6,7},{7,8},{8,9},{9,10},{10,1... | collective-permute-start | bytes 3145736 | tf_op jit(solution)/shard_map/while/body/eval_jaxpr/ppermute | solution.py:10
  249.7 20.4 %collective-permute-start = (f32[16,64,256]{2,1,0:T(8,128)}, f32[16,64,256]{2,1,0:T(8,128)S(1)}, u32[]{:S(2)}, u32[]{:S(2)}) collective-permute-start(f32[16,64,256]{2,1,0:T(8,128)} %multiply_add_fusion.5), channel_id=1, source_target_pairs={{0,1},{1,2},{2,3},{3,4},{4,5},{5,6},{6,7},{7,8},{8,9},{9,10},{10,1... | collective-permute-start | bytes 3145736 | tf_op jit(solution)/shard_map/while/body/eval_jaxpr/ppermute | solution.py:10
  271.3 20.4 %collective-permute-start = (f32[16,64,256]{2,1,0:T(8,128)}, f32[16,64,256]{2,1,0:T(8,128)S(1)}, u32[]{:S(2)}, u32[]{:S(2)}) collective-permute-start(f32[16,64,256]{2,1,0:T(8,128)} %multiply_add_fusion.5), channel_id=1, source_target_pairs={{0,1},{1,2},{2,3},{3,4},{4,5},{5,6},{6,7},{7,8},{8,9},{9,10},{10,1... | collective-permute-start | bytes 3145736 | tf_op jit(solution)/shard_map/while/body/eval_jaxpr/ppermute | solution.py:10
  292.9 20.4 %collective-permute-start = (f32[16,64,256]{2,1,0:T(8,128)}, f32[16,64,256]{2,1,0:T(8,128)S(1)}, u32[]{:S(2)}, u32[]{:S(2)}) collective-permute-start(f32[16,64,256]{2,1,0:T(8,128)} %multiply_add_fusion.5), channel_id=1, source_target_pairs={{0,1},{1,2},{2,3},{3,4},{4,5},{5,6},{6,7},{7,8},{8,9},{9,10},{10,1... | collective-permute-start | bytes 3145736 | tf_op jit(solution)/shard_map/while/body/eval_jaxpr/ppermute | solution.py:10
  314.5 21.1 %collective-permute-start = (f32[16,64,256]{2,1,0:T(8,128)}, f32[16,64,256]{2,1,0:T(8,128)S(1)}, u32[]{:S(2)}, u32[]{:S(2)}) collective-permute-start(f32[16,64,256]{2,1,0:T(8,128)} %multiply_add_fusion.5), channel_id=1, source_target_pairs={{0,1},{1,2},{2,3},{3,4},{4,5},{5,6},{6,7},{7,8},{8,9},{9,10},{10,1... | collective-permute-start | bytes 3145736 | tf_op jit(solution)/shard_map/while/body/eval_jaxpr/ppermute | solution.py:10
  336.8 21.9 %collective-permute-start = (f32[16,64,256]{2,1,0:T(8,128)}, f32[16,64,256]{2,1,0:T(8,128)S(1)}, u32[]{:S(2)}, u32[]{:S(2)}) collective-permute-start(f32[16,64,256]{2,1,0:T(8,128)} %multiply_add_fusion.5), channel_id=1, source_target_pairs={{0,1},{1,2},{2,3},{3,4},{4,5},{5,6},{6,7},{7,8},{8,9},{9,10},{10,1... | collective-permute-start | bytes 3145736 | tf_op jit(solution)/shard_map/while/body/eval_jaxpr/ppermute | solution.py:10
  359.9 22.7 %collective-permute-start = (f32[16,64,256]{2,1,0:T(8,128)}, f32[16,64,256]{2,1,0:T(8,128)S(1)}, u32[]{:S(2)}, u32[]{:S(2)}) collective-permute-start(f32[16,64,256]{2,1,0:T(8,128)} %multiply_add_fusion.5), channel_id=1, source_target_pairs={{0,1},{1,2},{2,3},{3,4},{4,5},{5,6},{6,7},{7,8},{8,9},{9,10},{10,1... | collective-permute-start | bytes 3145736 | tf_op jit(solution)/shard_map/while/body/eval_jaxpr/ppermute | solution.py:10
  382.7 52.8 %copy-start.3 = (s32[256,1]{0,1:T(1,128)S(1)}, s32[256,1]{0,1:T(1,128)}, u32[]{:S(2)}) copy-start(s32[256,1]{0,1:T(1,128)} %param.18) | copy-start | bytes 3076
  382.7 52.8 %copy-start.2 = (s32[256]{0:T(256)S(1)}, s32[256]{0:T(256)}, u32[]{:S(2)}) copy-start(s32[256]{0:T(256)} %param.19) | copy-start | bytes 3076
Sparse Core Ops, SparseCore 0:
  440.2 61.8 reduce-scatter.1
where the time goes:
time: 514 us; the launch traced here: 510 us
  waiting for transfers between devices  317 us (62%)
  starting transfers between devices  81 us (16%)
  blocking collectives  36 us (7%)
  other arithmetic  31 us (6%)
  matrix products  29 us (6%)
  between operations  13.5 us (3%)
    ppermute x15, waiting for transfers between devices, passed_along(): return lax.ppermute(block, axis, route)  255 us
    ppermute x15, starting transfers between devices, passed_along(): return lax.ppermute(block, axis, route)  81 us
    reduce_scatter x1, waiting for transfers between devices, per_device(): lax.psum_scatter(settings, 'feeder', scatter_dimension=0, tiled=True)  62 us
    all_gather x1, blocking collectives, per_device(): every_flow = lax.all_gather(head_flow, 'feeder', axis=0, tiled=True)  36 us
    add x15, other arithmetic, one_turn(): local_state + decay_prod[:, None, :] * incoming  17.6 us
    dot_general x1, matrix products, per_device(): jnp.einsum('fcts,fks->fktc', states, out_map, precision=lax.Precision.HIG...  16.8 us
  transfers between devices with their start and end apart: 16, of which 16 were waited for; matrix products, arithmetic and copies ran while one was open for 0% of the time, Pallas kernels for 0%

commit v1 on v0

v1 whole, which is shorter than its diff:
```python
import functools

import jax
import jax.numpy as jnp
from jax import lax
from jax.experimental import pallas as pl
from jax.experimental.pallas import tpu as pltpu
from jax.sharding import PartitionSpec as P

F32 = jnp.float32
BF16 = jnp.bfloat16
CAP = 2
NT = (((1,), (1,)), ((), ()))
NN = (((1,), (0,)), ((), ()))
WHOLE = pl.BlockSpec(memory_space=pltpu.VMEM)
SCALARS = pl.BlockSpec(memory_space=pltpu.SMEM)


def split(x):
    high = x.astype(BF16)
    return high, (x - high.astype(F32)).astype(BF16)


def dot(a, b, dims):
    return lax.dot_general(a, b, dims, preferred_element_type=F32)


def dot3(a, b, dims):
    a_high, a_low = split(a)
    b_high, b_low = split(b)
    rows = a.shape[0]
    both = dot(jnp.concatenate([a_high, a_low], 0), b_high, dims)
    return both[:rows] + both[rows:] + dot(a_high, b_low, dims)


def member_slots(areas, block):
    lane = lax.broadcasted_iota(jnp.int32, areas.shape, 1)
    within = lax.rem(lane, block)
    rank = jnp.zeros_like(areas)
    for back in range(1, block):
        same = (areas == pltpu.roll(areas, back, 1)) & (within >= back)
        rank = rank + same.astype(jnp.int32)
    return lax.div(lane, block) * CAP + rank


def drive_kernel(
    counts_ref, load_ref, map_ref, decay_ref, out_ref, area_ref, bus_ref, sens_ref,
    send_ref, flow_ref, sens_out_ref,
):
    step = pl.program_id(0)
    span, scen, nodes = load_ref.shape[1:]
    width = map_ref.shape[2]
    per_dev = decay_ref.shape[1]

    drive = dot(load_ref[0].reshape(span * scen, nodes), map_ref[0], NN)
    live = lax.broadcasted_iota(jnp.int32, (1, width), 1) < counts_ref[step]
    drive = jnp.where(live, drive, 0.0)
    state = drive[:scen]
    states = [state]
    retain = [decay_ref[t, pl.ds(step, 1), :] for t in range(span)]
    for t in range(1, span):
        state = retain[t] * state + drive[t * scen : (t + 1) * scen]
        states.append(state)
    send_ref[0, 0:scen] = state
    tail = send_ref.shape[1] - scen
    send_ref[0, scen:] = jnp.concatenate(
        retain + [jnp.zeros((tail - span, width), F32)], 0
    )
    flow = dot3(out_ref[0], jnp.concatenate(states, 0), NT)
    lanes = flow_ref.shape[2]
    planes = flow.shape[1] // lanes
    for k in range(2):
        for piece in range(planes):
            flow_ref[k * planes + piece, pl.ds(step, 1), :] = flow[
                k : k + 1, piece * lanes : (piece + 1) * lanes
            ]

    @pl.when(step == 0)
    def _():
        areas = area_ref[...]
        buses = bus_ref[...]
        count = areas.shape[1]
        bus_count = sens_ref.shape[2]
        blocks = count // per_dev
        members = blocks * CAP
        slots = member_slots(areas, per_dev)
        mine = areas == lax.axis_index("feeder")
        bus_hot = (
            lax.broadcasted_iota(jnp.int32, (bus_count, count), 0) == buses
        ).astype(BF16)
        row = lax.broadcasted_iota(jnp.int32, (members, count), 0)
        wanted = jnp.where(row < blocks, row * CAP, (row - blocks) * CAP + 1)
        by_rank = ((wanted == slots) & mine).astype(BF16)
        by_slot = ((row == slots) & mine).astype(BF16)
        row_bus = dot(by_rank, bus_hot, NT).astype(BF16)
        column_bus = dot(by_slot, bus_hot, NT).astype(BF16)
        parts = []
        for k in range(2):
            sens = sens_ref[0, k]
            high, low = split(sens)
            picked = dot(row_bus, high, NN) + dot(row_bus, low, NN)
            high, low = split(picked)
            parts.append(dot(high, column_bus, NT) + dot(low, column_bus, NT))
        sens_out_ref[...] = jnp.concatenate(
            [parts[k][s * blocks : (s + 1) * blocks] for s in range(CAP) for k in range(2)], 1
        )


def owner_kernel(recv_ref, out_ref, back_ref):
    chunks, rows, width = recv_ref.shape
    scen = back_ref.shape[2] // 2
    span = 6
    me = lax.axis_index("tm")
    out = out_ref[me]
    state = recv_ref[0, 0:scen]
    back_ref[0] = jnp.zeros(back_ref.shape[1:], F32)
    for chunk in range(1, chunks):
        product = recv_ref[chunk, scen : scen + 1]
        kept = [product]
        for t in range(1, span):
            product = product * recv_ref[chunk, scen + t : scen + t + 1]
            kept.append(product)
        blank = jnp.zeros((2, width), F32)
        even = [out[k : k + 1] * kept[t] for k in range(2) for t in range(0, span, 2)]
        odd = [out[k : k + 1] * kept[t] for k in range(2) for t in range(1, span, 2)]
        weights = jnp.concatenate(even + [blank] + odd + [blank], 0)
        flow = dot3(weights, state, NT)
        back_ref[chunk] = jnp.concatenate([flow[:8], flow[8:]], 1)
        if chunk < chunks - 1:
            state = recv_ref[chunk, 0:scen] + product * state


def join_kernel(back_ref, flow_ref, sens_ref, all_ref):
    planes, per_dev, lanes = flow_ref.shape
    stride = back_ref.shape[0] // per_dev
    for plane in range(planes):
        all_ref[plane] = flow_ref[plane] + back_ref[pl.ds(plane, per_dev, stride=stride), :]
    all_ref[planes] = sens_ref[...]


def mix_kernel(
    area_s, rule_s, knots_ref, levels_ref, area_ref, every_ref, result_ref,
    picked_ref, knot_ref, level_ref, own_ref,
):
    blocks, planes, per_dev, lanes = every_ref.shape
    planes = planes - 1
    count = blocks * per_dev
    me = lax.axis_index("feeder")
    areas = area_ref[...]
    slots = member_slots(areas, per_dev)
    for f in range(per_dev):
        area = area_s[me * per_dev + f]
        rank = jnp.int32(0)
        for earlier in range(f):
            rank = rank + jnp.where(area_s[me * per_dev + earlier] == area, 1, 0)
        row = every_ref[area, planes, pl.ds(me, 1), :]
        lane = lax.broadcasted_iota(jnp.int32, (1, lanes), 1)
        picked_ref[f : f + 1, :] = jnp.where(
            lax.div(lane, lanes // CAP) == rank, row, 0.0
        )
        rule = rule_s[me * per_dev + f]
        knot_ref[f : f + 1, :] = knots_ref[pl.ds(rule, 1), :].astype(F32) / 1000.0
        level_ref[f : f + 1, :] = levels_ref[pl.ds(rule, 1), :].astype(F32) / 1000.0
        own_ref[f : f + 1, :] = (areas == area).astype(F32)
    members = blocks * CAP
    lane = lax.broadcasted_iota(jnp.int32, (per_dev, lanes), 1)
    of_k = lax.rem(lax.div(lane, members), 2)
    picked = picked_ref[...]
    picked = jnp.concatenate([jnp.where(of_k == k, picked, 0.0) for k in range(2)], 0)
    spread = (
        lax.rem(lax.broadcasted_iota(jnp.int32, (lanes, count), 0), members) == slots
    ).astype(BF16)
    high, low = split(picked)
    weight = dot(high, spread, NN) + dot(low, spread, NN)
    own = own_ref[...]
    knot_volts = knot_ref[...]
    knot_levels = level_ref[...]
    per_k = planes // 2
    scen = result_ref.shape[2]
    weights = [weight[k * per_dev : (k + 1) * per_dev] * own for k in range(2)]
    for piece in range(per_k):
        volts = sum(
            dot3(weights[k], every_ref[:, k * per_k + piece].reshape(count, lanes), NN)
            for k in range(2)
        )
        result = knot_levels[:, 0:1] + jnp.zeros_like(volts)
        for j in range(knot_volts.shape[1] - 1):
            span_width = knot_volts[:, j + 1 : j + 2] - knot_volts[:, j : j + 1]
            slope = (knot_levels[:, j + 1 : j + 2] - knot_levels[:, j : j + 1]) / span_width
            result = result + slope * jnp.minimum(
                jnp.maximum(volts - knot_volts[:, j : j + 1], 0.0), span_width
            )
        result_ref[2 * piece] = result[:, :scen]
        result_ref[2 * piece + 1] = result[:, scen:]


def per_device(
    node_load, drive_map, decay_rate, counts, out_map, area_of, head_bus, rule_of,
    rule_knots, levels, sensitivity,
):
    per_dev, scen, span, nodes = node_load.shape
    width = drive_map.shape[2]
    feeders = area_of.shape[0]
    chunks = lax.axis_size("tm")
    blocks = lax.axis_size("feeder")
    rows = scen + 8
    lanes = 2 * scen
    planes = span
    load = jnp.transpose(node_load, (0, 2, 1, 3))
    decay = jnp.transpose(decay_rate, (1, 0, 2))
    area_row = jnp.transpose(area_of, (1, 0))
    bus_row = head_bus.reshape(1, feeders)

    send, flow, sens = pl.pallas_call(
        drive_kernel,
        grid=(per_dev,),
        in_specs=[
            SCALARS,
            pl.BlockSpec((1, span, scen, nodes), lambda f: (f, 0, 0, 0)),
            pl.BlockSpec((1, nodes, width), lambda f: (f, 0, 0)),
            pl.BlockSpec((span, per_dev, width), lambda f: (0, 0, 0)),
            pl.BlockSpec((1, 2, width), lambda f: (f, 0, 0)),
            pl.BlockSpec((1, feeders), lambda f: (0, 0)),
            pl.BlockSpec((1, feeders), lambda f: (0, 0)),
            pl.BlockSpec(sensitivity.shape, lambda f: (0, 0, 0, 0)),
        ],
        out_specs=[
            pl.BlockSpec((1, rows, width), lambda f: (f, 0, 0)),
            pl.BlockSpec((planes, per_dev, lanes), lambda f: (0, 0, 0)),
            pl.BlockSpec((per_dev, lanes), lambda f: (0, 0)),
        ],
        out_shape=[
            jax.ShapeDtypeStruct((per_dev, rows, width), F32),
            jax.ShapeDtypeStruct((planes, per_dev, lanes), F32),
            jax.ShapeDtypeStruct((per_dev, lanes), F32),
        ],
        compiler_params=pltpu.CompilerParams(vmem_limit_bytes=32 * 1024 * 1024),
        name="drive",
    )(counts, load, drive_map, decay, out_map, area_row, bus_row, sensitivity)

    owned = lax.all_to_all(send, "tm", 0, 0, tiled=True)
    back = pl.pallas_call(
        owner_kernel,
        in_specs=[WHOLE, WHOLE],
        out_specs=WHOLE,
        out_shape=jax.ShapeDtypeStruct((chunks, 8, lanes), F32),
        compiler_params=pltpu.CompilerParams(vmem_limit_bytes=16 * 1024 * 1024),
        name="owner",
    )(owned, out_map)
    back = lax.all_to_all(back, "tm", 0, 0, tiled=True)
    joined = pl.pallas_call(
        join_kernel,
        in_specs=[WHOLE] * 3,
        out_specs=WHOLE,
        out_shape=jax.ShapeDtypeStruct((planes + 1, per_dev, lanes), F32),
        name="join",
    )(back.reshape(per_dev * 8, lanes), flow, sens)
    every = lax.all_gather(joined, "feeder", axis=0, tiled=False)
    result = pl.pallas_call(
        mix_kernel,
        in_specs=[SCALARS, SCALARS, WHOLE, WHOLE, WHOLE, WHOLE],
        out_specs=WHOLE,
        out_shape=jax.ShapeDtypeStruct((span, per_dev, scen), F32),
        scratch_shapes=[
            pltpu.VMEM((per_dev, lanes), F32),
            pltpu.VMEM((per_dev, rule_knots.shape[1]), F32),
            pltpu.VMEM((per_dev, rule_knots.shape[1]), F32),
            pltpu.VMEM((per_dev, feeders), F32),
        ],
        compiler_params=pltpu.CompilerParams(vmem_limit_bytes=16 * 1024 * 1024),
        name="mix",
    )(area_of.reshape(feeders), rule_of, rule_knots, levels, area_row, every)
    return jnp.transpose(result, (1, 0, 2))


def solution(mesh):
    return jax.shard_map(
        per_device,
        mesh=mesh,
        in_specs=(
            P("feeder", None, "tm", None),
            P("feeder", None, None),
            P("feeder", "tm", None),
            P("feeder"),
            P("feeder", None, None),
            P(),
            P(),
            P(),
            P(),
            P(),
            P("feeder", None, None, None),
        ),
        out_specs=P("feeder", "tm", None),
        check_vma=False,
    )
```

time: 514 us -> 86.7 us (0.17)
  waiting for transfers between devices: 317 us -> 6.3 us
  starting transfers between devices: 81 us -> 3.5 us
  other arithmetic: 31 us -> 0 us
  matrix products: 29 us -> 0 us
  Pallas kernels: 0 us -> 15.1 us
  blocking collectives: 36 us -> 50.7 us
  between operations: 13.5 us -> 0.04 us
  local copies, waits for them, and re-layouts: 2.43 us -> 10.5 us
    ppermute x15 -> x0, waiting for transfers between devices: 255 us -> none  [passed_along(): return lax.ppermute(block, axis, route)]
    ppermute x15 -> x0, starting transfers between devices: 81 us -> none  [passed_along(): return lax.ppermute(block, axis, route)]
    reduce_scatter x1 -> x0, waiting for transfers between devices: 62 us -> none  [per_device(): lax.psum_scatter(settings, 'feeder', scatter_dimension=0, tiled=True)]
    dot_general x7 -> x0, matrix products: 29 us -> none  [the longest x1 16.8 us: per_device(): jnp.einsum('fcts,fks->fktc', states, out_map, precision=lax.Precision.HIG...]
    all_to_all x0 -> x1, blocking collectives: none -> 24.9 us  [per_device(): owned = lax.all_to_all(send, 'tm', 0, 0, tiled=True)]
    add x16 -> x0, other arithmetic: 18.5 us -> none  [the longest x15 17.6 us: one_turn(): local_state + decay_prod[:, None, :] * incoming]
    pallas_call x0 -> x4, Pallas kernels: none -> 15.1 us  [the longest x1 10.6 us: per_device(): pl.pallas_call(drive_kernel, grid=(per_dev,), in_specs=[SCALARS, pl.Block...]
    all_gather x1, blocking collectives: 36 us -> 25.8 us  [per_device(): every = lax.all_gather(joined, 'feeder', axis=0, tiled=False)]
  transfers between devices with their start and end apart: 16 -> 1, of which waited for: 16 -> 1; matrix products, arithmetic and copies ran while one was open for 0% -> 0% of each run, Pallas kernels for 0% -> 0%
where the time goes in v1:
time: 86.7 us; the launch traced here: 86.2 us
  blocking collectives  50.7 us (58%)
  Pallas kernels  15.1 us (17%)
  local copies, waits for them, and re-layouts  10.5 us (12%)
  waiting for transfers between devices  6.3 us (7%)
  starting transfers between devices  3.5 us (4%)
    all_gather x1, blocking collectives, per_device(): every = lax.all_gather(joined, 'feeder', axis=0, tiled=False)  25.8 us
    all_to_all x1, blocking collectives, per_device(): owned = lax.all_to_all(send, 'tm', 0, 0, tiled=True)  24.9 us
    pallas_call x1, Pallas kernels, per_device(): pl.pallas_call(drive_kernel, grid=(per_dev,), in_specs=[SCALARS, pl.Block...  10.6 us
    unnamed x32, local copies, waits for them, and re-layouts  10.5 us
    all_to_all x1, waiting for transfers between devices, per_device(): back = lax.all_to_all(back, 'tm', 0, 0, tiled=True)  6.3 us
    all_to_all x1, starting transfers between devices, per_device(): back = lax.all_to_all(back, 'tm', 0, 0, tiled=True)  3.5 us
    pallas_call x1, Pallas kernels, per_device(): pl.pallas_call(mix_kernel, in_specs=[SCALARS, SCALARS, WHOLE, WHOLE, WHOL...  1.88 us
  transfers between devices with their start and end apart: 1, of which 1 were waited for; matrix products, arithmetic and copies ran while one was open for 0% of the time, Pallas kernels for 0%

profile of v1, /device:TPU:1, one launch (start us, length us, event | category | flops | bytes accessed | tf_op | source)
XLA Modules:
  0.0 86.2 jit_solution(2400942845294585717)
XLA Ops:
  0.0 0.0 copy-start
  0.0 2.8 %copy-done = bf16[16,64,6,512]{3,1,2,0:T(8,128)(2,1)S(1)} copy-done((bf16[16,64,6,512]{3,1,2,0:T(8,128)(2,1)S(1)}, bf16[16,64,6,512]{3,1,2,0:T(8,128)(2,1)}, u32[]{:S(2)}) %copy-start) | copy-done | bytes 6291480
  2.8 0.0 copy-start.1
  2.8 2.2 %copy-done.1 = bf16[16,512,256]{2,1,0:T(8,128)(2,1)S(1)} copy-done((bf16[16,512,256]{2,1,0:T(8,128)(2,1)S(1)}, bf16[16,512,256]{2,1,0:T(8,128)(2,1)}, u32[]{:S(2)}) %copy-start.1) | copy-done | bytes 4194328
  5.0 0.0 copy-start.2
  5.0 1.0 %copy-done.2 = f32[1,2,256,256]{3,2,1,0:T(8,128)S(1)} copy-done((f32[1,2,256,256]{3,2,1,0:T(8,128)S(1)}, f32[1,2,256,256]{3,2,1,0:T(8,128)}, u32[]{:S(2)}) %copy-start.2) | copy-done | bytes 524312
  6.0 0.0 copy-start.3
  6.0 0.8 copy-done.3
  6.8 0.0 copy-start.4
  6.8 0.9 %copy-done.4 = f32[16,6,256]{2,0,1:T(8,128)S(1)} copy-done((f32[16,6,256]{2,0,1:T(8,128)S(1)}, f32[16,6,256]{2,0,1:T(8,128)}, u32[]{:S(2)}) %copy-start.4) | copy-done | bytes 98328
  7.7 0.0 copy-start.6
  7.7 0.7 copy-done.6
  8.3 0.7 copy-done.9
  9.0 0.7 copy-done.11
  9.7 10.6 %drive.1 = (f32[16,72,256]{2,1,0:T(8,128)S(1)}, f32[6,16,128]{2,1,0:T(8,128)S(1)}, f32[16,128]{1,0:T(8,128)S(1)}) custom-call(s32[16]{0:T(128)S(1)} %copy-done.11, bf16[16,6,64,512]{3,2,1,0:T(8,128)(2,1)S(1)} %bitcast.8, bf16[16,512,256]{2,1,0:T(8,128)(2,1)S(1)} %copy-done.1, f32[6,16,256]{2,1,0:T(8,128)S(1)} %bitcast.10, f32[16,2,256]{2,1,0:T(2,128)S(1)} %copy-done.3, ...), custom_call_target="tpu_custom_call" | custom-call | tf_op jit(solution)/shard_map/drive/pallas_call | solution.py:214
  20.3 0.0 copy-start.10
  20.3 24.9 %all_to_all.10.recv_ref = f32[16,72,256]{2,1,0:T(8,128)S(1)} all-to-all(f32[16,72,256]{2,1,0:T(8,128)S(1)} %get-tuple-element.8), channel_id=1, replica_groups=mesh['feeder'=16,'tm'=16] {'tm'}, dimensions={0} | all-to-all | bytes 2359296 | tf_op jit(solution)/shard_map/all_to_all | solution.py:241
  45.3 0.0 copy-done.5
  45.3 0.0 copy-done.8
  45.3 1.2 %owner.1 = f32[16,8,128]{2,1,0:T(8,128)} custom-call(f32[16,72,256]{2,1,0:T(8,128)S(1)} %all_to_all.10.recv_ref, f32[16,2,256]{2,1,0:T(2,128)S(1)} %copy-done.3), custom_call_target="tpu_custom_call" | custom-call | tf_op jit(solution)/shard_map/owner/pallas_call | solution.py:242
  46.4 3.5 %all-to-all-start.1 = ((f32[16,8,128]{2,1,0:T(8,128)}), f32[16,8,128]{2,1,0:T(8,128)S(1)}, u32[]{:S(2)}, u32[]{:S(2)}) async-start(f32[16,8,128]{2,1,0:T(8,128)} %owner.1), calls=%async_computation.1 | async-start | bytes 131072 | tf_op jit(solution)/shard_map/all_to_all | solution.py:250
  50.0 0.0 copy-done.13
  50.0 0.1 copy.14.knots_ref
  50.0 0.0 copy-done.14
  50.0 0.1 copy.15.levels_ref
  50.1 6.3 %all-to-all-done.1 = f32[16,8,128]{2,1,0:T(8,128)S(1)} async-done(((f32[16,8,128]{2,1,0:T(8,128)}), f32[16,8,128]{2,1,0:T(8,128)S(1)}, u32[]{:S(2)}, u32[]{:S(2)}) %all-to-all-start.1) | async-done | bytes 65568 | tf_op jit(solution)/shard_map/all_to_all | solution.py:250
  56.4 0.6 copy-done.12
  57.0 1.5 %join.1 = f32[7,16,128]{2,1,0:T(8,128)} custom-call(f32[128,128]{1,0:T(8,128)} %bitcast.15, f32[6,16,128]{2,1,0:T(8,128)} %copy-done.5, f32[16,128]{1,0:T(8,128)} %copy-done.8), custom_call_target="tpu_custom_call" | custom-call | tf_op jit(solution)/shard_map/join/pallas_call | solution.py:251
  58.5 25.8 %all-gather = f32[112,16,128]{2,1,0:T(8,128)S(1)} all-gather(f32[7,16,128]{2,1,0:T(8,128)} %join.1), channel_id=2, replica_groups=mesh['feeder'=16,'tm'=16] {'feeder'}, dimensions={0}, use_global_device_ids=true | all-gather | bytes 974848 | tf_op jit(solution)/shard_map/all_gather | solution.py:258
  84.3 0.0 copy-done.7
  84.3 0.0 copy-done.10
  84.3 1.9 %mix.1 = f32[6,16,64]{2,1,0:T(8,128)} custom-call(s32[256]{0:T(256)S(1)} %bitcast.12, s32[256]{0:T(256)S(1)} %copy-done.10, s32[16,8]{1,0:T(8,128)S(1)} %copy.14.knots_ref, s32[16,8]{1,0:T(8,128)S(1)} %copy.15.levels_ref, s32[1,256]{1,0:T(1,128)S(1)} %bitcast.13, f32[16,7,16,128]{3,2,1,0:T(8,128)S(1)} %bitcast.9), custom_call_target="tpu_custom_call" | custom-call | tf_op jit(solution)/shard_map/mix/pallas_call | solution.py:259
  (8 shorter events, 0.0 us)
Async XLA Ops:
  0.0 2.8 %copy-start = (bf16[16,64,6,512]{3,1,2,0:T(8,128)(2,1)S(1)}, bf16[16,64,6,512]{3,1,2,0:T(8,128)(2,1)}, u32[]{:S(2)}) copy-start(bf16[16,64,6,512]{3,1,2,0:T(8,128)(2,1)} %param.11) | copy-start | bytes 18874372
  2.8 2.2 %copy-start.1 = (bf16[16,512,256]{2,1,0:T(8,128)(2,1)S(1)}, bf16[16,512,256]{2,1,0:T(8,128)(2,1)}, u32[]{:S(2)}) copy-start(bf16[16,512,256]{2,1,0:T(8,128)(2,1)} %map_ref.1) | copy-start | bytes 12582916
  5.0 1.0 %copy-start.2 = (f32[1,2,256,256]{3,2,1,0:T(8,128)S(1)}, f32[1,2,256,256]{3,2,1,0:T(8,128)}, u32[]{:S(2)}) copy-start(f32[1,2,256,256]{3,2,1,0:T(8,128)} %sens_ref.1) | copy-start | bytes 1572868
  6.0 0.8 copy-start.3
  6.8 0.9 %copy-start.4 = (f32[16,6,256]{2,0,1:T(8,128)S(1)}, f32[16,6,256]{2,0,1:T(8,128)}, u32[]{:S(2)}) copy-start(f32[16,6,256]{2,0,1:T(8,128)} %param.13) | copy-start | bytes 294916
  7.7 0.7 copy-start.6
  8.3 0.7 copy-start.9
  9.0 0.7 copy-start.11
  9.7 40.3 %copy-start.13 = (s32[16,8]{0,1:T(8,128)S(1)}, s32[16,8]{0,1:T(8,128)}, u32[]{:S(2)}) copy-start(s32[16,8]{0,1:T(8,128)} %param.19) | copy-start | bytes 1540
  9.7 40.4 %copy-start.14 = (s32[16,8]{0,1:T(8,128)S(1)}, s32[16,8]{0,1:T(8,128)}, u32[]{:S(2)}) copy-start(s32[16,8]{0,1:T(8,128)} %param.20) | copy-start | bytes 1540
  20.3 25.0 %copy-start.5 = (f32[6,16,128]{2,1,0:T(8,128)}, f32[6,16,128]{2,1,0:T(8,128)S(1)}, u32[]{:S(2)}) copy-start(f32[6,16,128]{2,1,0:T(8,128)S(1)} %get-tuple-element.9.flow_ref) | copy-start | bytes 147460
  20.3 25.0 %copy-start.8 = (f32[16,128]{1,0:T(8,128)}, f32[16,128]{1,0:T(8,128)S(1)}, u32[]{:S(2)}) copy-start(f32[16,128]{1,0:T(8,128)S(1)} %get-tuple-element.10.sens_ref) | copy-start | bytes 24580
  20.3 64.0 %copy-start.7 = (s32[256,1]{0,1:T(1,128)S(1)}, s32[256,1]{0,1:T(1,128)}, u32[]{:S(2)}) copy-start(s32[256,1]{0,1:T(1,128)} %param.16) | copy-start | bytes 3076
  20.3 64.0 %copy-start.10 = (s32[256]{0:T(256)S(1)}, s32[256]{0:T(256)}, u32[]{:S(2)}) copy-start(s32[256]{0:T(256)} %rule_s.1) | copy-start | bytes 3076
  46.4 10.0 %all-to-all-start.1 = ((f32[16,8,128]{2,1,0:T(8,128)}), f32[16,8,128]{2,1,0:T(8,128)S(1)}, u32[]{:S(2)}, u32[]{:S(2)}) async-start(f32[16,8,128]{2,1,0:T(8,128)} %owner.1), calls=%async_computation.1 | async-start | bytes 131072 | tf_op jit(solution)/shard_map/all_to_all | solution.py:250
  56.4 0.6 copy-start.12

commit v2 on v1

--- a/solution.py
+++ b/solution.py
@@ -10,6 +10,7 @@
 F32 = jnp.float32
 BF16 = jnp.bfloat16
 CAP = 2
+GROUPS = (4, 4, 4, 4)
 NT = (((1,), (1,)), ((), ()))
 NN = (((1,), (0,)), ((), ()))
 WHOLE = pl.BlockSpec(memory_space=pltpu.VMEM)
@@ -43,67 +44,117 @@
     return lax.div(lane, block) * CAP + rank
 
 
+def area_matrix(areas, buses, sens_ref, per_dev):
+    count = areas.shape[1]
+    bus_count = sens_ref.shape[2]
+    blocks = count // per_dev
+    members = blocks * CAP
+    slots = member_slots(areas, per_dev)
+    mine = areas == lax.axis_index("feeder")
+    bus_hot = (lax.broadcasted_iota(jnp.int32, (bus_count, count), 0) == buses).astype(BF16)
+    row = lax.broadcasted_iota(jnp.int32, (members, count), 0)
+    wanted = jnp.where(row < blocks, row * CAP, (row - blocks) * CAP + 1)
+    by_rank = ((wanted == slots) & mine).astype(BF16)
+    by_slot = ((row == slots) & mine).astype(BF16)
+    row_bus = dot(by_rank, bus_hot, NT).astype(BF16)
+    column_bus = dot(by_slot, bus_hot, NT).astype(BF16)
+    parts = []
+    for k in range(2):
+        high, low = split(sens_ref[0, k])
+        picked = dot(row_bus, high, NN) + dot(row_bus, low, NN)
+        high, low = split(picked)
+        parts.append(dot(high, column_bus, NT) + dot(low, column_bus, NT))
+    return jnp.concatenate(
+        [parts[k][s * blocks : (s + 1) * blocks] for s in range(CAP) for k in range(2)], 1
+    )
+
+
 def drive_kernel(
-    counts_ref, load_ref, map_ref, decay_ref, out_ref, area_ref, bus_ref, sens_ref,
-    send_ref, flow_ref, sens_out_ref,
+    counts_hbm, load_hbm, map_hbm, decay_hbm, out_hbm, area_hbm, bus_hbm, sens_hbm,
+    send_hbm, flow_ref, sens_out_ref,
+    send_ref, counts_ref, load_ref, map_ref, decay_ref, out_ref, area_ref, bus_ref, sens_ref,
+    load_sems, map_sems, send_sems, sems,
 ):
-    step = pl.program_id(0)
-    span, scen, nodes = load_ref.shape[1:]
+    per_dev, span, scen, nodes = load_ref.shape
     width = map_ref.shape[2]
-    per_dev = decay_ref.shape[1]
-
-    drive = dot(load_ref[0].reshape(span * scen, nodes), map_ref[0], NN)
-    live = lax.broadcasted_iota(jnp.int32, (1, width), 1) < counts_ref[step]
-    drive = jnp.where(live, drive, 0.0)
-    state = drive[:scen]
-    states = [state]
-    retain = [decay_ref[t, pl.ds(step, 1), :] for t in range(span)]
-    for t in range(1, span):
-        state = retain[t] * state + drive[t * scen : (t + 1) * scen]
-        states.append(state)
-    send_ref[0, 0:scen] = state
-    tail = send_ref.shape[1] - scen
-    send_ref[0, scen:] = jnp.concatenate(
-        retain + [jnp.zeros((tail - span, width), F32)], 0
-    )
-    flow = dot3(out_ref[0], jnp.concatenate(states, 0), NT)
     lanes = flow_ref.shape[2]
-    planes = flow.shape[1] // lanes
-    for k in range(2):
-        for piece in range(planes):
-            flow_ref[k * planes + piece, pl.ds(step, 1), :] = flow[
-                k : k + 1, piece * lanes : (piece + 1) * lanes
+    small = [
+        pltpu.make_async_copy(source, target, sems.at[i])
+        for i, (source, target) in enumerate(
+            [
+                (area_hbm, area_ref),
+                (bus_hbm, bus_ref),
+                (sens_hbm, sens_ref),
+                (counts_hbm, counts_ref),
+                (decay_hbm, decay_ref),
+                (out_hbm, out_ref),
             ]
-
-    @pl.when(step == 0)
-    def _():
-        areas = area_ref[...]
-        buses = bus_ref[...]
-        count = areas.shape[1]
-        bus_count = sens_ref.shape[2]
-        blocks = count // per_dev
-        members = blocks * CAP
-        slots = member_slots(areas, per_dev)
-        mine = areas == lax.axis_index("feeder")
-        bus_hot = (
-            lax.broadcasted_iota(jnp.int32, (bus_count, count), 0) == buses
-        ).astype(BF16)
-        row = lax.broadcasted_iota(jnp.int32, (members, count), 0)
-        wanted = jnp.where(row < blocks, row * CAP, (row - blocks) * CAP + 1)
-        by_rank = ((wanted == slots) & mine).astype(BF16)
-        by_slot = ((row == slots) & mine).astype(BF16)
-        row_bus = dot(by_rank, bus_hot, NT).astype(BF16)
-        column_bus = dot(by_slot, bus_hot, NT).astype(BF16)
-        parts = []
+        )
+    ]
+    loads = [
+        pltpu.make_async_copy(load_hbm.at[f], load_ref.at[f], load_sems.at[f])
+        for f in range(per_dev)
+    ]
+    maps = [
+        pltpu.make_async_copy(map_hbm.at[f], map_ref.at[f], map_sems.at[f])
+        for f in range(per_dev)
+    ]
+    for copy in small:
+        copy.start()
+    for f in range(per_dev):
+        loads[f].start(priority=0)
+        maps[f].start(priority=1)
+    for copy in small:
+        copy.wait()
+    sens_out_ref[...] = area_matrix(area_ref[...], bus_ref[...], sens_ref, per_dev)
+    blank = jnp.zeros((send_ref.shape[1] - scen - span, width), F32)
+    lane = lax.broadcasted_iota(jnp.int32, (1, width), 1)
+    sends = [
+        pltpu.make_async_copy(send_ref.at[f], send_hbm.at[f], send_sems.at[f])
+        for f in range(per_dev)
+    ]
+
+    def record(f, drive):
+        drive = jnp.where(lane < counts_ref[f], drive, 0.0)
+        retain = [decay_ref[t, f : f + 1, :] for t in range(span)]
+        state = drive[:scen]
+        states = [state]
+        for t in range(1, span):
+            state = retain[t] * state + drive[t * scen : (t + 1) * scen]
+            states.append(state)
+        send_ref[f, 0:scen] = state
+        send_ref[f, scen:] = jnp.concatenate(retain + [blank], 0)
+        return jnp.concatenate(states, 0)
+
+    def project(f, states):
+        flow = dot3(out_ref[f], states, NT)
+        planes = flow.shape[1] // lanes
         for k in range(2):
-            sens = sens_ref[0, k]
-            high, low = split(sens)
-            picked = dot(row_bus, high, NN) + dot(row_bus, low, NN)
-            high, low = split(picked)
-            parts.append(dot(high, column_bus, NT) + dot(low, column_bus, NT))
-        sens_out_ref[...] = jnp.concatenate(
-            [parts[k][s * blocks : (s + 1) * blocks] for s in range(CAP) for k in range(2)], 1
-        )
+            for piece in range(planes):
+                flow_ref[k * planes + piece, f : f + 1, :] = flow[
+                    k : k + 1, piece * lanes : (piece + 1) * lanes
+                ]
+
+    groups, begin = [], 0
+    for size in GROUPS:
+        groups.append(range(begin, begin + size))
+        begin += size
+    before, drives = [], []
+    for group in groups + [[]]:
+        for f in group:
+            maps[f].wait()
+            loads[f].wait()
+        fresh = [
+            dot(load_ref[f].reshape(span * scen, nodes), map_ref[f], NN) for f in group
+        ]
+        histories = [record(f, drive) for f, drive in zip(before, drives)]
+        for f, history in zip(before, histories):
+            project(f, history)
+        for f in before:
+            sends[f].start()
+        before, drives = group, fresh
+    for copy in sends:
+        copy.wait()
 
 
 def owner_kernel(recv_ref, out_ref, back_ref):
@@ -194,6 +245,34 @@
         result_ref[2 * piece + 1] = result[:, scen:]
 
 
+def drive_call(counts, load, drive_map, decay, out_map, area_row, bus_row, sensitivity):
+    per_dev, span, scen, _ = load.shape
+    width = drive_map.shape[2]
+    rows, lanes = scen + 8, 2 * scen
+    operands = (load, drive_map, decay, out_map, area_row, bus_row, sensitivity)
+    return pl.pallas_call(
+        drive_kernel,
+        in_specs=[pl.BlockSpec(memory_space=pl.ANY)] * (1 + len(operands)),
+        out_specs=[pl.BlockSpec(memory_space=pl.ANY), WHOLE, WHOLE],
+        out_shape=[
+            jax.ShapeDtypeStruct((per_dev, rows, width), F32),
+            jax.ShapeDtypeStruct((span, per_dev, lanes), F32),
+            jax.ShapeDtypeStruct((per_dev, lanes), F32),
+        ],
+        scratch_shapes=[pltpu.VMEM((per_dev, rows, width), F32)]
+        + [pltpu.SMEM(counts.shape, counts.dtype)]
+        + [pltpu.VMEM(x.shape, x.dtype) for x in operands]
+        + [
+            pltpu.SemaphoreType.DMA((per_dev,)),
+            pltpu.SemaphoreType.DMA((per_dev,)),
+            pltpu.SemaphoreType.DMA((per_dev,)),
+            pltpu.SemaphoreType.DMA((6,)),
+        ],
+        compiler_params=pltpu.CompilerParams(vmem_limit_bytes=60 * 1024 * 1024),
+        name="drive",
+    )(counts, *operands)
+
+
 def per_device(
     node_load, drive_map, decay_rate, counts, out_map, area_of, head_bus, rule_of,
     rule_knots, levels, sensitivity,
@@ -211,33 +290,9 @@
     area_row = jnp.transpose(area_of, (1, 0))
     bus_row = head_bus.reshape(1, feeders)
 
-    send, flow, sens = pl.pallas_call(
-        drive_kernel,
-        grid=(per_dev,),
-        in_specs=[
-            SCALARS,
-            pl.BlockSpec((1, span, scen, nodes), lambda f: (f, 0, 0, 0)),
-            pl.BlockSpec((1, nodes, width), lambda f: (f, 0, 0)),
-            pl.BlockSpec((span, per_dev, width), lambda f: (0, 0, 0)),
-            pl.BlockSpec((1, 2, width), lambda f: (f, 0, 0)),
-            pl.BlockSpec((1, feeders), lambda f: (0, 0)),
-            pl.BlockSpec((1, feeders), lambda f: (0, 0)),
-            pl.BlockSpec(sensitivity.shape, lambda f: (0, 0, 0, 0)),
-        ],
-        out_specs=[
-            pl.BlockSpec((1, rows, width), lambda f: (f, 0, 0)),
-            pl.BlockSpec((planes, per_dev, lanes), lambda f: (0, 0, 0)),
-            pl.BlockSpec((per_dev, lanes), lambda f: (0, 0)),
-        ],
-        out_shape=[
-            jax.ShapeDtypeStruct((per_dev, rows, width), F32),
-            jax.ShapeDtypeStruct((planes, per_dev, lanes), F32),
-            jax.ShapeDtypeStruct((per_dev, lanes), F32),
-        ],
-        compiler_params=pltpu.CompilerParams(vmem_limit_bytes=32 * 1024 * 1024),
-        name="drive",
-    )(counts, load, drive_map, decay, out_map, area_row, bus_row, sensitivity)
-
+    send, flow, sens = drive_call(
+        counts, load, drive_map, decay, out_map, area_row, bus_row, sensitivity
+    )
     owned = lax.all_to_all(send, "tm", 0, 0, tiled=True)
     back = pl.pallas_call(
         owner_kernel,
@@ -253,6 +308,7 @@
         in_specs=[WHOLE] * 3,
         out_specs=WHOLE,
         out_shape=jax.ShapeDtypeStruct((planes + 1, per_dev, lanes), F32),
+        compiler_params=pltpu.CompilerParams(vmem_limit_bytes=8 * 1024 * 1024),
         name="join",
     )(back.reshape(per_dev * 8, lanes), flow, sens)
     every = lax.all_gather(joined, "feeder", axis=0, tiled=False)

time: 86.7 us -> 74.5 us (0.86)
  local copies, waits for them, and re-layouts: 10.5 us -> 1.66 us
  Pallas kernels: 15.1 us -> 12.1 us
    unnamed x32 -> x16, local copies, waits for them, and re-layouts: 10.5 us -> 1.66 us
    pallas_call x1, Pallas kernels: 10.6 us -> 9.06 us  [drive_call(): pl.pallas_call(drive_kernel, in_specs=[pl.BlockSpec(memory_space=pl.ANY)]...]
    pallas_call x1, Pallas kernels: 1.49 us -> 0.01 us  [per_device(): pl.pallas_call(join_kernel, in_specs=[WHOLE] * 3, out_specs=WHOLE, out_sh...]
where the time goes in v2:
time: 74.5 us; the launch traced here: 74.2 us
  blocking collectives  50.6 us (68%)
  Pallas kernels  12.1 us (16%)
  waiting for transfers between devices  6.3 us (8%)
  starting transfers between devices  3.48 us (5%)
  local copies, waits for them, and re-layouts  1.66 us (2%)
    all_gather x1, blocking collectives, per_device(): every = lax.all_gather(joined, 'feeder', axis=0, tiled=False)  25.6 us
    all_to_all x1, blocking collectives, per_device(): owned = lax.all_to_all(send, 'tm', 0, 0, tiled=True)  25 us
    pallas_call x1, Pallas kernels, drive_call(): pl.pallas_call(drive_kernel, in_specs=[pl.BlockSpec(memory_space=pl.ANY)]...  9.06 us
    all_to_all x1, waiting for transfers between devices, per_device(): back = lax.all_to_all(back, 'tm', 0, 0, tiled=True)  6.3 us
    all_to_all x1, starting transfers between devices, per_device(): back = lax.all_to_all(back, 'tm', 0, 0, tiled=True)  3.48 us
    pallas_call x1, Pallas kernels, per_device(): pl.pallas_call(mix_kernel, in_specs=[SCALARS, SCALARS, WHOLE, WHOLE, WHOL...  1.87 us
    unnamed x16, local copies, waits for them, and re-layouts  1.66 us
  transfers between devices with their start and end apart: 1, of which 1 were waited for; matrix products, arithmetic and copies ran while one was open for 0% of the time, Pallas kernels for 0%

profile of v2, /device:TPU:1, one launch (start us, length us, event | category | flops | bytes accessed | tf_op | source)
XLA Modules:
  0.0 74.2 jit_solution(7685456260021447645)
XLA Ops:
  0.0 0.0 copy-start
  0.0 0.0 copy-start.5
  0.0 0.0 copy-start.6
  0.0 9.1 %drive.1 = (f32[16,72,256]{2,1,0:T(8,128)}, f32[6,16,128]{2,1,0:T(8,128)}, f32[16,128]{1,0:T(8,128)}) custom-call(s32[16]{0:T(128)} %counts_hbm.1, bf16[16,6,64,512]{3,2,1,0:T(8,128)(2,1)} %bitcast.13, bf16[16,512,256]{2,1,0:T(8,128)(2,1)} %map_hbm.1, f32[6,16,256]{2,1,0:T(8,128)} %bitcast.14, f32[16,2,256]{2,1,0:T(2,128)} %out_ref.1, s32[1,256]{1,0:T(1,128)} %bitcast.10, ...), custom_call_target="tpu_custom_call" | custom-call | tf_op jit(solution)/shard_map/drive/pallas_call | solution.py:253
  9.1 0.0 copy-start.2
  9.1 0.0 copy-start.4
  9.1 25.0 %all_to_all.10.recv_ref = f32[16,72,256]{2,1,0:T(8,128)S(1)} all-to-all(f32[16,72,256]{2,1,0:T(8,128)} %get-tuple-element.8), channel_id=1, replica_groups=mesh['feeder'=16,'tm'=16] {'tm'}, dimensions={0} | all-to-all | bytes 2359296 | tf_op jit(solution)/shard_map/all_to_all | solution.py:296
  34.1 0.0 copy-done
  34.1 1.1 %owner.1 = f32[16,8,128]{2,1,0:T(8,128)} custom-call(f32[16,72,256]{2,1,0:T(8,128)S(1)} %all_to_all.10.recv_ref, f32[16,2,256]{2,1,0:T(2,128)S(1)} %copy-done), custom_call_target="tpu_custom_call" | custom-call | tf_op jit(solution)/shard_map/owner/pallas_call | solution.py:297
  35.3 3.5 %all-to-all-start.1 = ((f32[16,8,128]{2,1,0:T(8,128)}), f32[16,8,128]{2,1,0:T(8,128)S(1)}, u32[]{:S(2)}, u32[]{:S(2)}) async-start(f32[16,8,128]{2,1,0:T(8,128)} %owner.1), calls=%async_computation.1 | async-start | bytes 131072 | tf_op jit(solution)/shard_map/all_to_all | solution.py:305
  38.8 0.0 copy-done.5
  38.8 0.1 copy.14.knots_ref
  38.8 0.0 copy-done.6
  38.8 0.1 copy.15.levels_ref
  38.9 6.3 %all-to-all-done.1 = f32[16,8,128]{2,1,0:T(8,128)S(1)} async-done(((f32[16,8,128]{2,1,0:T(8,128)}), f32[16,8,128]{2,1,0:T(8,128)S(1)}, u32[]{:S(2)}, u32[]{:S(2)}) %all-to-all-start.1) | async-done | bytes 65568 | tf_op jit(solution)/shard_map/all_to_all | solution.py:305
  45.2 0.0 copy-start.1
  45.2 0.8 %copy-done.1 = f32[6,16,128]{2,1,0:T(8,128)S(1)} copy-done((f32[6,16,128]{2,1,0:T(8,128)S(1)}, f32[6,16,128]{2,1,0:T(8,128)}, u32[]{:S(2)}) %copy-start.1) | copy-done | bytes 49176
  46.0 0.0 copy-start.3
  46.0 0.7 copy-done.3
  46.7 25.6 %all-gather = f32[112,16,128]{2,1,0:T(8,128)S(1)} all-gather(f32[7,16,128]{2,1,0:T(8,128)S(1)} %join.1), channel_id=2, replica_groups=mesh['feeder'=16,'tm'=16] {'feeder'}, dimensions={0}, use_global_device_ids=true | all-gather | bytes 974848 | tf_op jit(solution)/shard_map/all_gather | solution.py:314
  72.3 0.0 copy-done.2
  72.3 0.0 copy-done.4
  72.3 1.9 %mix.1 = f32[6,16,64]{2,1,0:T(8,128)} custom-call(s32[256]{0:T(256)S(1)} %bitcast.11, s32[256]{0:T(256)S(1)} %copy-done.4, s32[16,8]{1,0:T(8,128)S(1)} %copy.14.knots_ref, s32[16,8]{1,0:T(8,128)S(1)} %copy.15.levels_ref, s32[1,256]{1,0:T(1,128)S(1)} %bitcast.12, f32[16,7,16,128]{3,2,1,0:T(8,128)S(1)} %bitcast.8), custom_call_target="tpu_custom_call" | custom-call | tf_op jit(solution)/shard_map/mix/pallas_call | solution.py:315
  (1 shorter events, 0.0 us)
Async XLA Ops:
  0.0 34.1 %copy-start = (f32[16,2,256]{2,1,0:T(2,128)S(1)}, f32[16,2,256]{2,1,0:T(2,128)}, u32[]{:S(2)}) copy-start(f32[16,2,256]{2,1,0:T(2,128)} %out_ref.1) | copy-start | bytes 98308
  0.0 38.8 %copy-start.5 = (s32[16,8]{0,1:T(8,128)S(1)}, s32[16,8]{0,1:T(8,128)}, u32[]{:S(2)}) copy-start(s32[16,8]{0,1:T(8,128)} %param.19) | copy-start | bytes 1540
  0.0 38.8 %copy-start.6 = (s32[16,8]{0,1:T(8,128)S(1)}, s32[16,8]{0,1:T(8,128)}, u32[]{:S(2)}) copy-start(s32[16,8]{0,1:T(8,128)} %param.20) | copy-start | bytes 1540
  9.1 63.2 %copy-start.2 = (s32[256,1]{0,1:T(1,128)S(1)}, s32[256,1]{0,1:T(1,128)}, u32[]{:S(2)}) copy-start(s32[256,1]{0,1:T(1,128)} %param.16) | copy-start | bytes 3076
  9.1 63.2 %copy-start.4 = (s32[256]{0:T(256)S(1)}, s32[256]{0:T(256)}, u32[]{:S(2)}) copy-start(s32[256]{0:T(256)} %rule_s.1) | copy-start | bytes 3076
  35.3 9.9 %all-to-all-start.1 = ((f32[16,8,128]{2,1,0:T(8,128)}), f32[16,8,128]{2,1,0:T(8,128)S(1)}, u32[]{:S(2)}, u32[]{:S(2)}) async-start(f32[16,8,128]{2,1,0:T(8,128)} %owner.1), calls=%async_computation.1 | async-start | bytes 131072 | tf_op jit(solution)/shard_map/all_to_all | solution.py:305
  45.2 0.8 %copy-start.1 = (f32[6,16,128]{2,1,0:T(8,128)S(1)}, f32[6,16,128]{2,1,0:T(8,128)}, u32[]{:S(2)}) copy-start(f32[6,16,128]{2,1,0:T(8,128)} %get-tuple-element.9.flow_ref) | copy-start | bytes 147460
  46.0 0.7 copy-start.3

commit v3 on v2

v3 whole, which is shorter than its diff:
```python
import functools

import jax
import jax.numpy as jnp
from jax import lax
from jax.experimental import pallas as pl
from jax.experimental.pallas import tpu as pltpu
from jax.sharding import PartitionSpec as P

F32 = jnp.float32
BF16 = jnp.bfloat16
CAP = 2
OWN, MASKS, HOT, SLOT, KNOT, SLOPE = range(6)
GROUPS = (4, 4, 4, 4)
NT = (((1,), (1,)), ((), ()))
NN = (((1,), (0,)), ((), ()))
WHOLE = pl.BlockSpec(memory_space=pltpu.VMEM)
ANYWHERE = pl.BlockSpec(memory_space=pl.ANY)


def split(x):
    high = x.astype(BF16)
    return high, (x - high.astype(F32)).astype(BF16)


def dot(a, b, dims):
    return lax.dot_general(a, b, dims, preferred_element_type=F32)


def dot3(a, b, dims):
    a_high, a_low = split(a)
    b_high, b_low = split(b)
    rows = a.shape[0]
    both = dot(jnp.concatenate([a_high, a_low], 0), b_high, dims)
    return both[:rows] + both[rows:] + dot(a_high, b_low, dims)


def member_slots(areas, block):
    lane = lax.broadcasted_iota(jnp.int32, areas.shape, 1)
    within = lax.rem(lane, block)
    rank = jnp.zeros_like(areas)
    for back in range(1, block):
        same = (areas == pltpu.roll(areas, back, 1)) & (within >= back)
        rank = rank + same.astype(jnp.int32)
    return lax.div(lane, block) * CAP + rank, rank


def area_matrix(areas, slots, buses, sens_ref, per_dev):
    count = areas.shape[1]
    bus_count = sens_ref.shape[2]
    blocks = count // per_dev
    members = blocks * CAP
    mine = areas == lax.axis_index("feeder")
    bus_hot = (lax.broadcasted_iota(jnp.int32, (bus_count, count), 0) == buses).astype(BF16)
    row = lax.broadcasted_iota(jnp.int32, (members, count), 0)
    wanted = jnp.where(row < blocks, row * CAP, (row - blocks) * CAP + 1)
    by_rank = ((wanted == slots) & mine).astype(BF16)
    by_slot = ((row == slots) & mine).astype(BF16)
    row_bus = dot(by_rank, bus_hot, NT).astype(BF16)
    column_bus = dot(by_slot, bus_hot, NT).astype(BF16)
    parts = []
    for k in range(2):
        high, low = split(sens_ref[0, k])
        picked = dot(row_bus, high, NN) + dot(row_bus, low, NN)
        high, low = split(picked)
        parts.append(dot(high, column_bus, NT) + dot(low, column_bus, NT))
    return jnp.concatenate(
        [parts[k][s * blocks : (s + 1) * blocks] for s in range(CAP) for k in range(2)], 1
    )


def drives_of(group, load_ref, map_ref):
    per_dev, span, scen, nodes = load_ref.shape
    return [dot(load_ref[f].reshape(span * scen, nodes), map_ref[f], NN) for f in group]


def states_of(f, drive, live_count, decay_ref):
    span = decay_ref.shape[0]
    scen = drive.shape[0] // span
    lane = lax.broadcasted_iota(jnp.int32, (1, drive.shape[1]), 1)
    drive = jnp.where(lane < live_count, drive, 0.0)
    state = drive[:scen]
    states = [state]
    for t in range(1, span):
        state = decay_ref[t, f : f + 1, :] * state + drive[t * scen : (t + 1) * scen]
        states.append(state)
    return states


def started(pairs, sems):
    copies = [
        pltpu.make_async_copy(source, target, sems.at[i])
        for i, (source, target) in enumerate(pairs)
    ]
    for copy in copies:
        copy.start()
    return copies


def started_feeders(load_hbm, load_ref, load_sems, map_hbm, map_ref, map_sems):
    per_dev = load_ref.shape[0]
    loads = [
        pltpu.make_async_copy(load_hbm.at[f], load_ref.at[f], load_sems.at[f])
        for f in range(per_dev)
    ]
    maps = [
        pltpu.make_async_copy(map_hbm.at[f], map_ref.at[f], map_sems.at[f])
        for f in range(per_dev)
    ]
    for f in range(per_dev):
        loads[f].start(priority=0)
        maps[f].start(priority=1)
    return loads, maps


def groups_of(sizes):
    groups, begin = [], 0
    for size in sizes:
        groups.append(range(begin, begin + size))
        begin += size
    return groups


def drive_kernel(
    counts_hbm, load_hbm, map_hbm, decay_hbm,
    send_ref,
    counts_ref, load_ref, map_ref, decay_ref,
    load_sems, map_sems, sems,
):
    per_dev, span, scen, nodes = load_ref.shape
    width = map_ref.shape[2]
    small = started([(counts_hbm, counts_ref), (decay_hbm, decay_ref)], sems)
    loads, maps = started_feeders(load_hbm, load_ref, load_sems, map_hbm, map_ref, map_sems)
    for copy in small:
        copy.wait()
    blank = jnp.zeros((send_ref.shape[1] - scen - span, width), F32)
    before, drives = [], []
    for group in groups_of(GROUPS) + [[]]:
        for f in group:
            maps[f].wait()
            loads[f].wait()
        fresh = drives_of(group, load_ref, map_ref)
        for f, drive in zip(before, drives):
            send_ref[f, 0:scen] = states_of(f, drive, counts_ref[f], decay_ref)[-1]
            send_ref[f, scen:] = jnp.concatenate(
                [decay_ref[t, f : f + 1, :] for t in range(span)] + [blank], 0
            )
        before, drives = group, fresh


def side_kernel(
    counts_hbm, load_hbm, map_hbm, decay_hbm, out_hbm, area_ref, bus_ref, rule_ref, sens_hbm,
    knots_ref, levels_ref,
    flow_ref, table_ref,
    counts_ref, load_ref, map_ref, decay_ref, out_ref, sens_ref,
    load_sems, map_sems, sems,
):
    per_dev, span, scen, nodes = load_ref.shape
    lanes = flow_ref.shape[2]
    small = started(
        [
            (counts_hbm, counts_ref),
            (decay_hbm, decay_ref),
            (out_hbm, out_ref),
            (sens_hbm, sens_ref),
        ],
        sems,
    )
    loads, maps = started_feeders(load_hbm, load_ref, load_sems, map_hbm, map_ref, map_sems)
    areas = area_ref[...]
    rules = rule_ref[...]
    count = areas.shape[1]
    blocks = count // per_dev
    members = blocks * CAP
    slots, ranks = member_slots(areas, per_dev)
    me = lax.axis_index("feeder")
    feeder = lax.broadcasted_iota(jnp.int32, (per_dev, count), 1)
    here = feeder == me * per_dev + lax.broadcasted_iota(jnp.int32, (per_dev, count), 0)
    my_area = jnp.sum(jnp.where(here, areas, 0), axis=1, keepdims=True)
    my_rank = jnp.sum(jnp.where(here, ranks, 0), axis=1, keepdims=True)
    my_rule = jnp.sum(jnp.where(here, rules, 0), axis=1, keepdims=True)
    choice = lax.broadcasted_iota(jnp.int32, (per_dev, blocks), 1)
    hot = (choice == my_area).astype(F32)
    own = (areas == my_area).astype(F32)
    lane = lax.broadcasted_iota(jnp.int32, (per_dev, lanes), 1)
    of_rank = lax.div(lane, lanes // CAP) == my_rank
    of_k = lax.rem(lax.div(lane, members), 2)
    masks = [(of_rank & (of_k == k)).astype(F32) for k in range(2)]
    rule_count = knots_ref.shape[1]
    rule_choice = lax.broadcasted_iota(jnp.int32, (per_dev, rule_count), 1)
    rule_hot = (rule_choice == my_rule).astype(BF16)
    knots = knots_ref.shape[0]

    def looked_up(table_ref):
        high, low = split(table_ref[...].astype(F32))
        return (dot(rule_hot, high, NT) + dot(rule_hot, low, NT)) / 1000.0

    knot_volts = looked_up(knots_ref)
    knot_levels = looked_up(levels_ref)
    width = knot_volts[:, 1:] - knot_volts[:, : knots - 1]
    slope = (knot_levels[:, 1:] - knot_levels[:, : knots - 1]) / width
    table_ref[OWN, :, :] = own
    for k in range(2):
        table_ref[MASKS, :, k * lanes : (k + 1) * lanes] = masks[k]
    table_ref[HOT, :, :blocks] = hot
    table_ref[SLOT, :, :] = slots.astype(F32) + jnp.zeros((per_dev, count), F32)
    table_ref[KNOT, :, :knots] = knot_volts
    table_ref[KNOT, :, lanes : lanes + 1] = knot_levels[:, 0:1]
    table_ref[SLOPE, :, : knots - 1] = width
    table_ref[SLOPE, :, lanes : lanes + knots - 1] = slope
    for copy in small:
        copy.wait()
    planes = flow_ref.shape[0] - 1
    flow_ref[planes] = area_matrix(areas, slots, bus_ref[...], sens_ref, per_dev)
    for group in groups_of(GROUPS):
        for f in group:
            maps[f].wait()
            loads[f].wait()
        drives = drives_of(group, load_ref, map_ref)
        histories = [
            states_of(f, drive, counts_ref[f], decay_ref) for f, drive in zip(group, drives)
        ]
        for f, history in zip(group, histories):
            flow = dot3(out_ref[f], jnp.concatenate(history, 0), NT)
            for k in range(2):
                for piece in range(planes // 2):
                    flow_ref[k * (planes // 2) + piece, f : f + 1, :] = flow[
                        k : k + 1, piece * lanes : (piece + 1) * lanes
                    ]


def owner_kernel(recv_ref, out_ref, back_ref):
    chunks, rows, width = recv_ref.shape
    scen = back_ref.shape[2] // 2
    span = 6
    me = lax.axis_index("tm")
    out = out_ref[me]
    state = recv_ref[0, 0:scen]
    back_ref[0] = jnp.zeros(back_ref.shape[1:], F32)
    for chunk in range(1, chunks):
        product = recv_ref[chunk, scen : scen + 1]
        kept = [product]
        for t in range(1, span):
            product = product * recv_ref[chunk, scen + t : scen + t + 1]
            kept.append(product)
        blank = jnp.zeros((2, width), F32)
        even = [out[k : k + 1] * kept[t] for k in range(2) for t in range(0, span, 2)]
        odd = [out[k : k + 1] * kept[t] for k in range(2) for t in range(1, span, 2)]
        weights = jnp.concatenate(even + [blank] + odd + [blank], 0)
        flow = dot3(weights, state, NT)
        back_ref[chunk] = jnp.concatenate([flow[:8], flow[8:]], 1)
        if chunk < chunks - 1:
            state = recv_ref[chunk, 0:scen] + product * state


def join_kernel(back_ref, flow_ref, all_ref):
    planes, per_dev, lanes = flow_ref.shape
    stride = back_ref.shape[0] // per_dev
    for plane in range(planes - 1):
        all_ref[plane] = flow_ref[plane] + back_ref[pl.ds(plane, per_dev, stride=stride), :]
    all_ref[planes - 1] = flow_ref[planes - 1]


def mix_kernel(knots, table_ref, every_ref, result_ref):
    blocks, planes, per_dev, lanes = every_ref.shape
    planes = planes - 1
    count = blocks * per_dev
    members = blocks * CAP
    me = lax.axis_index("feeder")
    hot = table_ref[HOT, :, :blocks].astype(BF16)
    masks = [
        table_ref[MASKS, :, k * lanes : (k + 1) * lanes].astype(BF16) for k in range(2)
    ]
    row = lax.rem(lax.broadcasted_iota(jnp.int32, (lanes, count), 0), members)
    spread = (row.astype(F32) == table_ref[SLOT, 0:1, :]).astype(BF16)
    high, low = split(every_ref[:, planes, pl.ds(me, 1), :].reshape(blocks, lanes))
    weight = jnp.zeros((2 * per_dev, count), F32)
    for part in (high, low):
        picked = dot(hot, part, NN).astype(BF16)
        weight = weight + dot(
            jnp.concatenate([picked * masks[0], picked * masks[1]], 0), spread, NN
        )
    own = table_ref[OWN]
    weights = [weight[k * per_dev : (k + 1) * per_dev] * own for k in range(2)]
    per_k = planes // 2
    scen = result_ref.shape[2]
    knot_volts = table_ref[KNOT, :, :knots]
    first = table_ref[KNOT, :, lanes : lanes + 1]
    widths = table_ref[SLOPE, :, : knots - 1]
    slopes = table_ref[SLOPE, :, lanes : lanes + knots - 1]
    for piece in range(per_k):
        volts = sum(
            dot3(weights[k], every_ref[:, k * per_k + piece].reshape(count, lanes), NN)
            for k in range(2)
        )
        result = first + jnp.zeros_like(volts)
        for j in range(knots - 1):
            result = result + slopes[:, j : j + 1] * jnp.minimum(
                jnp.maximum(volts - knot_volts[:, j : j + 1], 0.0), widths[:, j : j + 1]
            )
        result_ref[2 * piece] = result[:, :scen]
        result_ref[2 * piece + 1] = result[:, scen:]


def drive_call(counts, load, drive_map, decay):
    per_dev, span, scen, _ = load.shape
    width = drive_map.shape[2]
    rows = scen + 8
    operands = (load, drive_map, decay)
    return pl.pallas_call(
        drive_kernel,
        in_specs=[ANYWHERE] * 4,
        out_specs=WHOLE,
        out_shape=pltpu.VMEM((per_dev, rows, width), F32),
        scratch_shapes=[pltpu.SMEM(counts.shape, counts.dtype)]
        + [pltpu.VMEM(x.shape, x.dtype) for x in operands]
        + [pltpu.SemaphoreType.DMA((per_dev,))] * 2
        + [pltpu.SemaphoreType.DMA((2,))],
        compiler_params=pltpu.CompilerParams(vmem_limit_bytes=58 * 1024 * 1024),
        name="drive",
    )(counts, *operands)


def side_call(
    counts, load, drive_map, decay, out_map, area_row, bus_row, rule_row, sensitivity,
    knots, levels,
):
    per_dev, span, scen, nodes = load.shape
    width = drive_map.shape[2]
    lanes = 2 * scen
    count = area_row.shape[1]
    shapes = [(span + 1, per_dev, lanes), (6, per_dev, count)]
    copied = (load, drive_map, decay, out_map, sensitivity)
    return pl.pallas_call(
        side_kernel,
        in_specs=[ANYWHERE] * 5 + [WHOLE] * 3 + [ANYWHERE] + [WHOLE] * 2,
        out_specs=[WHOLE] * len(shapes),
        out_shape=[pltpu.VMEM(shape, F32) for shape in shapes],
        scratch_shapes=[pltpu.SMEM(counts.shape, counts.dtype)]
        + [pltpu.VMEM(x.shape, x.dtype) for x in copied]
        + [pltpu.SemaphoreType.DMA((per_dev,))] * 2
        + [pltpu.SemaphoreType.DMA((4,))],
        compiler_params=pltpu.CompilerParams(vmem_limit_bytes=56 * 1024 * 1024),
        cost_estimate=pl.CostEstimate(
            flops=2 * per_dev * span * scen * nodes * width,
            bytes_accessed=20 * 1024 * 1024,
            transcendentals=0,
        ),
        name="side",
    )(
        counts, load, drive_map, decay, out_map, area_row, bus_row, rule_row, sensitivity,
        knots, levels,
    )


def per_device(
    node_load, drive_map, decay_rate, counts, out_map, area_of, head_bus, rule_of,
    rule_knots, levels, sensitivity,
):
    per_dev, scen, span, nodes = node_load.shape
    feeders = area_of.shape[0]
    chunks = lax.axis_size("tm")
    lanes = 2 * scen
    load = jnp.transpose(node_load, (0, 2, 1, 3))
    decay = jnp.transpose(decay_rate, (1, 0, 2))

    send = drive_call(counts, load, drive_map, decay)
    owned = lax.all_to_all(send, "tm", 0, 0, tiled=True)
    flow, table = side_call(
        counts, load, drive_map, decay, out_map,
        jnp.transpose(area_of, (1, 0)), head_bus.reshape(1, feeders),
        rule_of.reshape(1, feeders), sensitivity,
        jnp.transpose(rule_knots, (1, 0)), jnp.transpose(levels, (1, 0)),
    )
    owned, flow, table = lax.optimization_barrier((owned, flow, table))
    back = pl.pallas_call(
        owner_kernel,
        in_specs=[WHOLE, WHOLE],
        out_specs=WHOLE,
        out_shape=pltpu.VMEM((chunks, 8, lanes), F32),
        compiler_params=pltpu.CompilerParams(vmem_limit_bytes=16 * 1024 * 1024),
        name="owner",
    )(owned, out_map)
    back = lax.all_to_all(back, "tm", 0, 0, tiled=True)
    joined = pl.pallas_call(
        join_kernel,
        in_specs=[WHOLE] * 2,
        out_specs=WHOLE,
        out_shape=pltpu.VMEM(flow.shape, F32),
        compiler_params=pltpu.CompilerParams(vmem_limit_bytes=8 * 1024 * 1024),
        name="join",
    )(back.reshape(per_dev * 8, lanes), flow)
    every = lax.all_gather(joined, "feeder", axis=0, tiled=False)
    result = pl.pallas_call(
        functools.partial(mix_kernel, levels.shape[1]),
        in_specs=[WHOLE] * 2,
        out_specs=WHOLE,
        out_shape=jax.ShapeDtypeStruct((span, per_dev, scen), F32),
        compiler_params=pltpu.CompilerParams(vmem_limit_bytes=16 * 1024 * 1024),
        name="mix",
    )(table, every)
    return jnp.transpose(result, (1, 0, 2))


def solution(mesh):
    return jax.shard_map(
        per_device,
        mesh=mesh,
        in_specs=(
            P("feeder", None, "tm", None),
            P("feeder", None, None),
            P("feeder", "tm", None),
            P("feeder"),
            P("feeder", None, None),
            P(),
            P(),
            P(),
            P(),
            P(),
            P("feeder", None, None, None),
        ),
        out_specs=P("feeder", "tm", None),
        check_vma=False,
    )
```

time: 74.5 us -> 69.6 us (0.934)
  blocking collectives: 50.6 us -> 35.6 us
  Pallas kernels: 12.1 us -> 17.6 us
  starting transfers between devices: 3.48 us -> 7.6 us
  waiting for transfers between devices: 6.3 us -> 8.55 us
  local copies, waits for them, and re-layouts: 1.66 us -> 0.01 us
    all_to_all x1, blocking collectives: 25 us -> 11.3 us  [per_device(): back = lax.all_to_all(back, 'tm', 0, 0, tiled=True)]
    pallas_call x3 -> x4, Pallas kernels: 10.9 us -> 17.1 us  [the longest x1 8.83 us: side_call(): pl.pallas_call(side_kernel, in_specs=[ANYWHERE] * 5 + [WHOLE] * 3 + [ANYW...]
    all_to_all x1, starting transfers between devices: 3.48 us -> 7.6 us  [per_device(): owned = lax.all_to_all(send, 'tm', 0, 0, tiled=True)]
    all_to_all x1, waiting for transfers between devices: 6.3 us -> 8.55 us  [per_device(): owned = lax.all_to_all(send, 'tm', 0, 0, tiled=True)]
    unnamed x16 -> x2, local copies, waits for them, and re-layouts: 1.66 us -> 0.01 us
    all_gather x1, blocking collectives: 25.6 us -> 24.3 us  [per_device(): every = lax.all_gather(joined, 'feeder', axis=0, tiled=False)]
  transfers between devices with their start and end apart: 1 -> 1, of which waited for: 1 -> 1; matrix products, arithmetic and copies ran while one was open for 0% -> 0% of each run, Pallas kernels for 0% -> 13%
where the time goes in v3:
time: 69.6 us; the launch traced here: 69.4 us
  blocking collectives  35.6 us (51%)
  Pallas kernels  17.6 us (25%)
  waiting for transfers between devices  8.55 us (12%)
  starting transfers between devices  7.6 us (11%)
    all_gather x1, blocking collectives, per_device(): every = lax.all_gather(joined, 'feeder', axis=0, tiled=False)  24.3 us
    all_to_all x1, blocking collectives, per_device(): back = lax.all_to_all(back, 'tm', 0, 0, tiled=True)  11.3 us
    pallas_call x1, Pallas kernels, side_call(): pl.pallas_call(side_kernel, in_specs=[ANYWHERE] * 5 + [WHOLE] * 3 + [ANYW...  8.83 us
    all_to_all x1, waiting for transfers between devices, per_device(): owned = lax.all_to_all(send, 'tm', 0, 0, tiled=True)  8.55 us
    all_to_all x1, starting transfers between devices, per_device(): owned = lax.all_to_all(send, 'tm', 0, 0, tiled=True)  7.6 us
    pallas_call x1, Pallas kernels, drive_call(): pl.pallas_call(drive_kernel, in_specs=[ANYWHERE] * 4, out_specs=WHOLE, ou...  7.04 us
  transfers between devices with their start and end apart: 1, of which 1 were waited for; matrix products, arithmetic and copies ran while one was open for 0% of the time, Pallas kernels for 13%

profile of v3, /device:TPU:1, one launch (start us, length us, event | category | flops | bytes accessed | tf_op | source)
XLA Modules:
  0.0 69.4 jit_solution(18098004164425698600)
XLA Ops:
  0.0 7.0 %drive.1 = f32[16,72,256]{2,1,0:T(8,128)} custom-call(s32[16]{0:T(128)} %counts_hbm.3, bf16[16,6,64,512]{3,2,1,0:T(8,128)(2,1)} %bitcast.12, bf16[16,512,256]{2,1,0:T(8,128)(2,1)} %map_hbm.3, f32[6,16,256]{2,1,0:T(8,128)} %bitcast.14), custom_call_target="tpu_custom_call" | custom-call | tf_op jit(solution)/shard_map/drive/pallas_call | solution.py:310
  7.1 7.6 %all-to-all-start = ((f32[16,72,256]{2,1,0:T(8,128)}), f32[16,72,256]{2,1,0:T(8,128)S(1)}, u32[]{:S(2)}, u32[]{:S(2)}) async-start(f32[16,72,256]{2,1,0:T(8,128)} %drive.1), calls=%async_computation | async-start | bytes 2359296 | tf_op jit(solution)/shard_map/all_to_all | solution.py:368
  14.7 0.0 copy-start
  14.7 8.8 %side.1 = (f32[7,16,128]{2,1,0:T(8,128)S(1)}, f32[6,16,256]{2,1,0:T(8,128)S(1)}) custom-call(s32[16]{0:T(128)} %counts_hbm.3, bf16[16,6,64,512]{3,2,1,0:T(8,128)(2,1)} %bitcast.13, bf16[16,512,256]{2,1,0:T(8,128)(2,1)} %map_hbm.3, f32[6,16,256]{2,1,0:T(8,128)} %bitcast.15, f32[16,2,256]{2,1,0:T(2,128)} %out_ref.1, s32[1,256]{1,0:T(1,128)} %bitcast.18, ...), custom_call_target="tpu_custom_call" | custom-call | flops 1610612736 | bytes 20971520 | tf_op jit(solution)/shard_map/side/pallas_call | solution.py:334
  23.5 8.5 %all-to-all-done.recv_ref = f32[16,72,256]{2,1,0:T(8,128)S(1)} async-done(((f32[16,72,256]{2,1,0:T(8,128)}), f32[16,72,256]{2,1,0:T(8,128)S(1)}, u32[]{:S(2)}, u32[]{:S(2)}) %all-to-all-start) | async-done | bytes 1179680 | tf_op jit(solution)/shard_map/all_to_all | solution.py:368
  32.1 0.0 copy-done
  32.1 0.5 owner.1
  32.5 11.3 %all_to_all.10 = f32[16,8,128]{2,1,0:T(8,128)S(1)} all-to-all(f32[16,8,128]{2,1,0:T(8,128)S(1)} %owner.1), channel_id=1, replica_groups=mesh['feeder'=16,'tm'=16] {'tm'}, dimensions={0} | all-to-all | bytes 131072 | tf_op jit(solution)/shard_map/all_to_all | solution.py:384
  43.9 24.3 %all-gather = f32[112,16,128]{2,1,0:T(8,128)S(1)} all-gather(f32[7,16,128]{2,1,0:T(8,128)S(1)} %join.1), channel_id=2, replica_groups=mesh['feeder'=16,'tm'=16] {'feeder'}, dimensions={0}, use_global_device_ids=true | all-gather | bytes 974848 | tf_op jit(solution)/shard_map/all_gather | solution.py:393
  68.1 1.2 %mix.1 = f32[6,16,64]{2,1,0:T(8,128)} custom-call(f32[6,16,256]{2,1,0:T(8,128)S(1)} %get-tuple-element.12.table_ref, f32[16,7,16,128]{3,2,1,0:T(8,128)S(1)} %bitcast.10), custom_call_target="tpu_custom_call" | custom-call | tf_op jit(solution)/shard_map/mix/pallas_call | solution.py:394
  (1 shorter events, 0.0 us)
Async XLA Ops:
  7.1 25.0 %all-to-all-start = ((f32[16,72,256]{2,1,0:T(8,128)}), f32[16,72,256]{2,1,0:T(8,128)S(1)}, u32[]{:S(2)}, u32[]{:S(2)}) async-start(f32[16,72,256]{2,1,0:T(8,128)} %drive.1), calls=%async_computation | async-start | bytes 2359296 | tf_op jit(solution)/shard_map/all_to_all | solution.py:368
  14.7 17.4 %copy-start = (f32[16,2,256]{2,1,0:T(2,128)S(1)}, f32[16,2,256]{2,1,0:T(2,128)}, u32[]{:S(2)}) copy-start(f32[16,2,256]{2,1,0:T(2,128)} %out_ref.1) | copy-start | bytes 98308

commit v4 on v3

--- a/solution.py
+++ b/solution.py
@@ -11,7 +11,7 @@
 BF16 = jnp.bfloat16
 CAP = 2
 OWN, MASKS, HOT, SLOT, KNOT, SLOPE = range(6)
-GROUPS = (4, 4, 4, 4)
+GROUPS = (6, 6, 4)
 NT = (((1,), (1,)), ((), ()))
 NN = (((1,), (0,)), ((), ()))
 WHOLE = pl.BlockSpec(memory_space=pltpu.VMEM)
@@ -74,11 +74,9 @@
     return [dot(load_ref[f].reshape(span * scen, nodes), map_ref[f], NN) for f in group]
 
 
-def states_of(f, drive, live_count, decay_ref):
+def states_of(f, drive, decay_ref):
     span = decay_ref.shape[0]
     scen = drive.shape[0] // span
-    lane = lax.broadcasted_iota(jnp.int32, (1, drive.shape[1]), 1)
-    drive = jnp.where(lane < live_count, drive, 0.0)
     state = drive[:scen]
     states = [state]
     for t in range(1, span):
@@ -123,9 +121,9 @@
 
 def drive_kernel(
     counts_hbm, load_hbm, map_hbm, decay_hbm,
-    send_ref,
-    counts_ref, load_ref, map_ref, decay_ref,
-    load_sems, map_sems, sems,
+    send_hbm,
+    send_ref, counts_ref, load_ref, map_ref, decay_ref,
+    load_sems, map_sems, send_sems, sems,
 ):
     per_dev, span, scen, nodes = load_ref.shape
     width = map_ref.shape[2]
@@ -134,18 +132,27 @@
     for copy in small:
         copy.wait()
     blank = jnp.zeros((send_ref.shape[1] - scen - span, width), F32)
-    before, drives = [], []
-    for group in groups_of(GROUPS) + [[]]:
+    sends = [
+        pltpu.make_async_copy(send_ref.at[f], send_hbm.at[f], send_sems.at[f])
+        for f in range(per_dev)
+    ]
+    state_id = lax.broadcasted_iota(jnp.int32, (1, width), 1)
+    for group in groups_of(GROUPS):
         for f in group:
             maps[f].wait()
             loads[f].wait()
-        fresh = drives_of(group, load_ref, map_ref)
-        for f, drive in zip(before, drives):
-            send_ref[f, 0:scen] = states_of(f, drive, counts_ref[f], decay_ref)[-1]
+        drives = drives_of(group, load_ref, map_ref)
+        for f, drive in zip(group, drives):
+            send_ref[f, 0:scen] = jnp.where(
+                state_id < counts_ref[f], states_of(f, drive, decay_ref)[-1], 0.0
+            )
             send_ref[f, scen:] = jnp.concatenate(
                 [decay_ref[t, f : f + 1, :] for t in range(span)] + [blank], 0
             )
-        before, drives = group, fresh
+        for f in group:
+            sends[f].start()
+    for copy in sends:
+        copy.wait()
 
 
 def side_kernel(
@@ -212,16 +219,16 @@
         copy.wait()
     planes = flow_ref.shape[0] - 1
     flow_ref[planes] = area_matrix(areas, slots, bus_ref[...], sens_ref, per_dev)
+    state_id = lax.broadcasted_iota(jnp.int32, (1, map_ref.shape[2]), 1)
     for group in groups_of(GROUPS):
         for f in group:
             maps[f].wait()
             loads[f].wait()
         drives = drives_of(group, load_ref, map_ref)
-        histories = [
-            states_of(f, drive, counts_ref[f], decay_ref) for f, drive in zip(group, drives)
-        ]
+        histories = [states_of(f, drive, decay_ref) for f, drive in zip(group, drives)]
         for f, history in zip(group, histories):
-            flow = dot3(out_ref[f], jnp.concatenate(history, 0), NT)
+            out = jnp.where(state_id < counts_ref[f], out_ref[f], 0.0)
+            flow = dot3(out, jnp.concatenate(history, 0), NT)
             for k in range(2):
                 for piece in range(planes // 2):
                     flow_ref[k * (planes // 2) + piece, f : f + 1, :] = flow[
@@ -254,11 +261,10 @@
 
 
 def join_kernel(back_ref, flow_ref, all_ref):
-    planes, per_dev, lanes = flow_ref.shape
-    stride = back_ref.shape[0] // per_dev
-    for plane in range(planes - 1):
-        all_ref[plane] = flow_ref[plane] + back_ref[pl.ds(plane, per_dev, stride=stride), :]
-    all_ref[planes - 1] = flow_ref[planes - 1]
+    planes = flow_ref.shape[0] - 1
+    for plane in range(planes):
+        all_ref[plane] = flow_ref[plane] + back_ref[:, plane, :]
+    all_ref[planes] = flow_ref[planes]
 
 
 def mix_kernel(knots, table_ref, every_ref, result_ref):
@@ -310,11 +316,14 @@
     return pl.pallas_call(
         drive_kernel,
         in_specs=[ANYWHERE] * 4,
-        out_specs=WHOLE,
-        out_shape=pltpu.VMEM((per_dev, rows, width), F32),
-        scratch_shapes=[pltpu.SMEM(counts.shape, counts.dtype)]
+        out_specs=ANYWHERE,
+        out_shape=jax.ShapeDtypeStruct((per_dev, rows, width), F32),
+        scratch_shapes=[
+            pltpu.VMEM((per_dev, rows, width), F32),
+            pltpu.SMEM(counts.shape, counts.dtype),
+        ]
         + [pltpu.VMEM(x.shape, x.dtype) for x in operands]
-        + [pltpu.SemaphoreType.DMA((per_dev,))] * 2
+        + [pltpu.SemaphoreType.DMA((per_dev,))] * 3
         + [pltpu.SemaphoreType.DMA((2,))],
         compiler_params=pltpu.CompilerParams(vmem_limit_bytes=58 * 1024 * 1024),
         name="drive",
@@ -389,7 +398,7 @@
         out_shape=pltpu.VMEM(flow.shape, F32),
         compiler_params=pltpu.CompilerParams(vmem_limit_bytes=8 * 1024 * 1024),
         name="join",
-    )(back.reshape(per_dev * 8, lanes), flow)
+    )(back, flow)
     every = lax.all_gather(joined, "feeder", axis=0, tiled=False)
     result = pl.pallas_call(
         functools.partial(mix_kernel, levels.shape[1]),

time: 69.6 us -> 69.2 us (level)
  Pallas kernels: 17.6 us -> 16.9 us
  transfers between devices with their start and end apart: 1 -> 1, of which waited for: 1 -> 1; matrix products, arithmetic and copies ran while one was open for 0% -> 0% of each run, Pallas kernels for 13% -> 12%
where the time goes in v4:
time: 69.2 us; the launch traced here: 68.9 us
  blocking collectives  35.6 us (51%)
  Pallas kernels  16.9 us (24%)
  waiting for transfers between devices  8.77 us (13%)
  starting transfers between devices  7.6 us (11%)
    all_gather x1, blocking collectives, per_device(): every = lax.all_gather(joined, 'feeder', axis=0, tiled=False)  24.3 us
    all_to_all x1, blocking collectives, per_device(): back = lax.all_to_all(back, 'tm', 0, 0, tiled=True)  11.3 us
    all_to_all x1, waiting for transfers between devices, per_device(): owned = lax.all_to_all(send, 'tm', 0, 0, tiled=True)  8.77 us
    pallas_call x1, Pallas kernels, side_call(): pl.pallas_call(side_kernel, in_specs=[ANYWHERE] * 5 + [WHOLE] * 3 + [ANYW...  8.6 us
    all_to_all x1, starting transfers between devices, per_device(): owned = lax.all_to_all(send, 'tm', 0, 0, tiled=True)  7.6 us
    pallas_call x1, Pallas kernels, drive_call(): pl.pallas_call(drive_kernel, in_specs=[ANYWHERE] * 4, out_specs=ANYWHERE,...  6.57 us
  transfers between devices with their start and end apart: 1, of which 1 were waited for; matrix products, arithmetic and copies ran while one was open for 0% of the time, Pallas kernels for 12%

profile of v4, /device:TPU:1, one launch (start us, length us, event | category | flops | bytes accessed | tf_op | source)
XLA Modules:
  0.0 68.9 jit_solution(9000235332997444239)
XLA Ops:
  0.0 6.6 %drive.1 = f32[16,72,256]{2,1,0:T(8,128)} custom-call(s32[16]{0:T(128)} %counts_hbm.3, bf16[16,6,64,512]{3,2,1,0:T(8,128)(2,1)} %bitcast.10, bf16[16,512,256]{2,1,0:T(8,128)(2,1)} %map_hbm.3, f32[6,16,256]{2,1,0:T(8,128)} %bitcast.12), custom_call_target="tpu_custom_call" | custom-call | tf_op jit(solution)/shard_map/drive/pallas_call | solution.py:316
  6.6 7.6 %all-to-all-start = ((f32[16,72,256]{2,1,0:T(8,128)}), f32[16,72,256]{2,1,0:T(8,128)S(1)}, u32[]{:S(2)}, u32[]{:S(2)}) async-start(f32[16,72,256]{2,1,0:T(8,128)} %drive.1), calls=%async_computation | async-start | bytes 2359296 | tf_op jit(solution)/shard_map/all_to_all | solution.py:377
  14.2 0.0 copy-start
  14.2 8.6 %side.1 = (f32[7,16,128]{2,1,0:T(8,128)S(1)}, f32[6,16,256]{2,1,0:T(8,128)S(1)}) custom-call(s32[16]{0:T(128)} %counts_hbm.3, bf16[16,6,64,512]{3,2,1,0:T(8,128)(2,1)} %bitcast.11, bf16[16,512,256]{2,1,0:T(8,128)(2,1)} %map_hbm.3, f32[6,16,256]{2,1,0:T(8,128)} %bitcast.13, f32[16,2,256]{2,1,0:T(2,128)} %out_ref.1, s32[1,256]{1,0:T(1,128)} %bitcast.16, ...), custom_call_target="tpu_custom_call" | custom-call | flops 1610612736 | bytes 20971520 | tf_op jit(solution)/shard_map/side/pallas_call | solution.py:343
  22.8 8.8 %all-to-all-done.recv_ref = f32[16,72,256]{2,1,0:T(8,128)S(1)} async-done(((f32[16,72,256]{2,1,0:T(8,128)}), f32[16,72,256]{2,1,0:T(8,128)S(1)}, u32[]{:S(2)}, u32[]{:S(2)}) %all-to-all-start) | async-done | bytes 1179680 | tf_op jit(solution)/shard_map/all_to_all | solution.py:377
  31.6 0.0 copy-done
  31.6 0.5 owner.1
  32.1 11.3 %all_to_all.10.back_ref = f32[16,8,128]{2,1,0:T(8,128)S(1)} all-to-all(f32[16,8,128]{2,1,0:T(8,128)S(1)} %owner.1), channel_id=1, replica_groups=mesh['feeder'=16,'tm'=16] {'tm'}, dimensions={0} | all-to-all | bytes 131072 | tf_op jit(solution)/shard_map/all_to_all | solution.py:393
  43.4 24.3 %all-gather = f32[112,16,128]{2,1,0:T(8,128)S(1)} all-gather(f32[7,16,128]{2,1,0:T(8,128)S(1)} %join.1), channel_id=2, replica_groups=mesh['feeder'=16,'tm'=16] {'feeder'}, dimensions={0}, use_global_device_ids=true | all-gather | bytes 974848 | tf_op jit(solution)/shard_map/all_gather | solution.py:402
  67.7 1.2 %mix.1 = f32[6,16,64]{2,1,0:T(8,128)} custom-call(f32[6,16,256]{2,1,0:T(8,128)S(1)} %get-tuple-element.12.table_ref, f32[16,7,16,128]{3,2,1,0:T(8,128)S(1)} %bitcast.9), custom_call_target="tpu_custom_call" | custom-call | tf_op jit(solution)/shard_map/mix/pallas_call | solution.py:403
  (1 shorter events, 0.0 us)
Async XLA Ops:
  6.6 25.0 %all-to-all-start = ((f32[16,72,256]{2,1,0:T(8,128)}), f32[16,72,256]{2,1,0:T(8,128)S(1)}, u32[]{:S(2)}, u32[]{:S(2)}) async-start(f32[16,72,256]{2,1,0:T(8,128)} %drive.1), calls=%async_computation | async-start | bytes 2359296 | tf_op jit(solution)/shard_map/all_to_all | solution.py:377
  14.2 17.4 %copy-start = (f32[16,2,256]{2,1,0:T(2,128)S(1)}, f32[16,2,256]{2,1,0:T(2,128)}, u32[]{:S(2)}) copy-start(f32[16,2,256]{2,1,0:T(2,128)} %out_ref.1) | copy-start | bytes 98308

commit v5 on v4

--- a/solution.py
+++ b/solution.py
@@ -106,8 +106,8 @@
         for f in range(per_dev)
     ]
     for f in range(per_dev):
-        loads[f].start(priority=0)
-        maps[f].start(priority=1)
+        loads[f].start(priority=1)
+        maps[f].start(priority=0)
     return loads, maps
 
 

time: 69.2 us -> 68.8 us (level)
  Pallas kernels: 16.9 us -> 15.9 us
where the time goes in v5:
time: 68.8 us; the launch traced here: 68.5 us
  blocking collectives  35.6 us (52%)
  Pallas kernels  15.9 us (23%)
  waiting for transfers between devices  9.33 us (14%)
  starting transfers between devices  7.59 us (11%)
    all_gather x1, blocking collectives, per_device(): every = lax.all_gather(joined, 'feeder', axis=0, tiled=False)  24.3 us
    all_to_all x1, blocking collectives, per_device(): back = lax.all_to_all(back, 'tm', 0, 0, tiled=True)  11.3 us
    all_to_all x1, waiting for transfers between devices, per_device(): owned = lax.all_to_all(send, 'tm', 0, 0, tiled=True)  9.33 us
    pallas_call x1, Pallas kernels, side_call(): pl.pallas_call(side_kernel, in_specs=[ANYWHERE] * 5 + [WHOLE] * 3 + [ANYW...  8.04 us
    all_to_all x1, starting transfers between devices, per_device(): owned = lax.all_to_all(send, 'tm', 0, 0, tiled=True)  7.59 us
    pallas_call x1, Pallas kernels, drive_call(): pl.pallas_call(drive_kernel, in_specs=[ANYWHERE] * 4, out_specs=ANYWHERE,...  6.19 us
  transfers between devices with their start and end apart: 1, of which 1 were waited for; matrix products, arithmetic and copies ran while one was open for 0% of the time, Pallas kernels for 12%

profile of v5, /device:TPU:1, one launch (start us, length us, event | category | flops | bytes accessed | tf_op | source)
XLA Modules:
  0.0 68.5 jit_solution(12164539596878343094)
XLA Ops:
  0.0 6.2 %drive.1 = f32[16,72,256]{2,1,0:T(8,128)} custom-call(s32[16]{0:T(128)} %counts_hbm.3, bf16[16,6,64,512]{3,2,1,0:T(8,128)(2,1)} %bitcast.10, bf16[16,512,256]{2,1,0:T(8,128)(2,1)} %map_hbm.3, f32[6,16,256]{2,1,0:T(8,128)} %bitcast.12), custom_call_target="tpu_custom_call" | custom-call | tf_op jit(solution)/shard_map/drive/pallas_call | solution.py:316
  6.2 7.6 %all-to-all-start = ((f32[16,72,256]{2,1,0:T(8,128)}), f32[16,72,256]{2,1,0:T(8,128)S(1)}, u32[]{:S(2)}, u32[]{:S(2)}) async-start(f32[16,72,256]{2,1,0:T(8,128)} %drive.1), calls=%async_computation | async-start | bytes 2359296 | tf_op jit(solution)/shard_map/all_to_all | solution.py:377
  13.8 0.0 copy-start
  13.8 8.0 %side.1 = (f32[7,16,128]{2,1,0:T(8,128)S(1)}, f32[6,16,256]{2,1,0:T(8,128)S(1)}) custom-call(s32[16]{0:T(128)} %counts_hbm.3, bf16[16,6,64,512]{3,2,1,0:T(8,128)(2,1)} %bitcast.11, bf16[16,512,256]{2,1,0:T(8,128)(2,1)} %map_hbm.3, f32[6,16,256]{2,1,0:T(8,128)} %bitcast.13, f32[16,2,256]{2,1,0:T(2,128)} %out_ref.1, s32[1,256]{1,0:T(1,128)} %bitcast.16, ...), custom_call_target="tpu_custom_call" | custom-call | flops 1610612736 | bytes 20971520 | tf_op jit(solution)/shard_map/side/pallas_call | solution.py:343
  21.9 9.3 %all-to-all-done.recv_ref = f32[16,72,256]{2,1,0:T(8,128)S(1)} async-done(((f32[16,72,256]{2,1,0:T(8,128)}), f32[16,72,256]{2,1,0:T(8,128)S(1)}, u32[]{:S(2)}, u32[]{:S(2)}) %all-to-all-start) | async-done | bytes 1179680 | tf_op jit(solution)/shard_map/all_to_all | solution.py:377
  31.2 0.0 copy-done
  31.2 0.5 owner.1
  31.7 11.3 %all_to_all.10.back_ref = f32[16,8,128]{2,1,0:T(8,128)S(1)} all-to-all(f32[16,8,128]{2,1,0:T(8,128)S(1)} %owner.1), channel_id=1, replica_groups=mesh['feeder'=16,'tm'=16] {'tm'}, dimensions={0} | all-to-all | bytes 131072 | tf_op jit(solution)/shard_map/all_to_all | solution.py:393
  43.1 24.3 %all-gather = f32[112,16,128]{2,1,0:T(8,128)S(1)} all-gather(f32[7,16,128]{2,1,0:T(8,128)S(1)} %join.1), channel_id=2, replica_groups=mesh['feeder'=16,'tm'=16] {'feeder'}, dimensions={0}, use_global_device_ids=true | all-gather | bytes 974848 | tf_op jit(solution)/shard_map/all_gather | solution.py:402
  67.3 1.2 %mix.1 = f32[6,16,64]{2,1,0:T(8,128)} custom-call(f32[6,16,256]{2,1,0:T(8,128)S(1)} %get-tuple-element.12.table_ref, f32[16,7,16,128]{3,2,1,0:T(8,128)S(1)} %bitcast.9), custom_call_target="tpu_custom_call" | custom-call | tf_op jit(solution)/shard_map/mix/pallas_call | solution.py:403
  (1 shorter events, 0.0 us)
Async XLA Ops:
  6.2 25.0 %all-to-all-start = ((f32[16,72,256]{2,1,0:T(8,128)}), f32[16,72,256]{2,1,0:T(8,128)S(1)}, u32[]{:S(2)}, u32[]{:S(2)}) async-start(f32[16,72,256]{2,1,0:T(8,128)} %drive.1), calls=%async_computation | async-start | bytes 2359296 | tf_op jit(solution)/shard_map/all_to_all | solution.py:377
  13.8 17.4 %copy-start = (f32[16,2,256]{2,1,0:T(2,128)S(1)}, f32[16,2,256]{2,1,0:T(2,128)}, u32[]{:S(2)}) copy-start(f32[16,2,256]{2,1,0:T(2,128)} %out_ref.1) | copy-start | bytes 98308

commit v6 on v5

--- a/solution.py
+++ b/solution.py
@@ -131,7 +131,6 @@
     loads, maps = started_feeders(load_hbm, load_ref, load_sems, map_hbm, map_ref, map_sems)
     for copy in small:
         copy.wait()
-    blank = jnp.zeros((send_ref.shape[1] - scen - span, width), F32)
     sends = [
         pltpu.make_async_copy(send_ref.at[f], send_hbm.at[f], send_sems.at[f])
         for f in range(per_dev)
@@ -147,7 +146,7 @@
                 state_id < counts_ref[f], states_of(f, drive, decay_ref)[-1], 0.0
             )
             send_ref[f, scen:] = jnp.concatenate(
-                [decay_ref[t, f : f + 1, :] for t in range(span)] + [blank], 0
+                [decay_ref[t, f : f + 1, :] for t in range(span)], 0
             )
         for f in group:
             sends[f].start()
@@ -311,7 +310,7 @@
 def drive_call(counts, load, drive_map, decay):
     per_dev, span, scen, _ = load.shape
     width = drive_map.shape[2]
-    rows = scen + 8
+    rows = scen + span
     operands = (load, drive_map, decay)
     return pl.pallas_call(
         drive_kernel,

time: 68.8 us -> 68.8 us (level)
  no operation moved by 1% of the time
where the time goes in v6:
time: 68.8 us; the launch traced here: 68.5 us
  blocking collectives  35.6 us (52%)
  Pallas kernels  15.9 us (23%)
  waiting for transfers between devices  9.33 us (14%)
  starting transfers between devices  7.59 us (11%)
    all_gather x1, blocking collectives, per_device(): every = lax.all_gather(joined, 'feeder', axis=0, tiled=False)  24.3 us
    all_to_all x1, blocking collectives, per_device(): back = lax.all_to_all(back, 'tm', 0, 0, tiled=True)  11.3 us
    all_to_all x1, waiting for transfers between devices, per_device(): owned = lax.all_to_all(send, 'tm', 0, 0, tiled=True)  9.33 us
    pallas_call x1, Pallas kernels, side_call(): pl.pallas_call(side_kernel, in_specs=[ANYWHERE] * 5 + [WHOLE] * 3 + [ANYW...  8.04 us
    all_to_all x1, starting transfers between devices, per_device(): owned = lax.all_to_all(send, 'tm', 0, 0, tiled=True)  7.59 us
    pallas_call x1, Pallas kernels, drive_call(): pl.pallas_call(drive_kernel, in_specs=[ANYWHERE] * 4, out_specs=ANYWHERE,...  6.19 us
  transfers between devices with their start and end apart: 1, of which 1 were waited for; matrix products, arithmetic and copies ran while one was open for 0% of the time, Pallas kernels for 12%

profile of v6, /device:TPU:1, one launch (start us, length us, event | category | flops | bytes accessed | tf_op | source)
XLA Modules:
  0.0 68.5 jit_solution(16913422317022917312)
XLA Ops:
  0.0 6.2 %drive.1 = f32[16,70,256]{2,1,0:T(8,128)} custom-call(s32[16]{0:T(128)} %counts_hbm.3, bf16[16,6,64,512]{3,2,1,0:T(8,128)(2,1)} %bitcast.10, bf16[16,512,256]{2,1,0:T(8,128)(2,1)} %map_hbm.3, f32[6,16,256]{2,1,0:T(8,128)} %bitcast.12), custom_call_target="tpu_custom_call" | custom-call | tf_op jit(solution)/shard_map/drive/pallas_call | solution.py:315
  6.2 7.6 %all-to-all-start = ((f32[16,70,256]{2,1,0:T(8,128)}), f32[16,70,256]{2,1,0:T(8,128)S(1)}, u32[]{:S(2)}, u32[]{:S(2)}) async-start(f32[16,70,256]{2,1,0:T(8,128)} %drive.1), calls=%async_computation | async-start | bytes 2359296 | tf_op jit(solution)/shard_map/all_to_all | solution.py:376
  13.8 0.0 copy-start
  13.8 8.0 %side.1 = (f32[7,16,128]{2,1,0:T(8,128)S(1)}, f32[6,16,256]{2,1,0:T(8,128)S(1)}) custom-call(s32[16]{0:T(128)} %counts_hbm.3, bf16[16,6,64,512]{3,2,1,0:T(8,128)(2,1)} %bitcast.11, bf16[16,512,256]{2,1,0:T(8,128)(2,1)} %map_hbm.3, f32[6,16,256]{2,1,0:T(8,128)} %bitcast.13, f32[16,2,256]{2,1,0:T(2,128)} %out_ref.1, s32[1,256]{1,0:T(1,128)} %bitcast.16, ...), custom_call_target="tpu_custom_call" | custom-call | flops 1610612736 | bytes 20971520 | tf_op jit(solution)/shard_map/side/pallas_call | solution.py:342
  21.9 9.3 %all-to-all-done.recv_ref = f32[16,70,256]{2,1,0:T(8,128)S(1)} async-done(((f32[16,70,256]{2,1,0:T(8,128)}), f32[16,70,256]{2,1,0:T(8,128)S(1)}, u32[]{:S(2)}, u32[]{:S(2)}) %all-to-all-start) | async-done | bytes 1146912 | tf_op jit(solution)/shard_map/all_to_all | solution.py:376
  31.2 0.0 copy-done
  31.2 0.5 owner.1
  31.7 11.3 %all_to_all.10.back_ref = f32[16,8,128]{2,1,0:T(8,128)S(1)} all-to-all(f32[16,8,128]{2,1,0:T(8,128)S(1)} %owner.1), channel_id=1, replica_groups=mesh['feeder'=16,'tm'=16] {'tm'}, dimensions={0} | all-to-all | bytes 131072 | tf_op jit(solution)/shard_map/all_to_all | solution.py:392
  43.1 24.3 %all-gather = f32[112,16,128]{2,1,0:T(8,128)S(1)} all-gather(f32[7,16,128]{2,1,0:T(8,128)S(1)} %join.1), channel_id=2, replica_groups=mesh['feeder'=16,'tm'=16] {'feeder'}, dimensions={0}, use_global_device_ids=true | all-gather | bytes 974848 | tf_op jit(solution)/shard_map/all_gather | solution.py:401
  67.3 1.2 %mix.1 = f32[6,16,64]{2,1,0:T(8,128)} custom-call(f32[6,16,256]{2,1,0:T(8,128)S(1)} %get-tuple-element.12.table_ref, f32[16,7,16,128]{3,2,1,0:T(8,128)S(1)} %bitcast.9), custom_call_target="tpu_custom_call" | custom-call | tf_op jit(solution)/shard_map/mix/pallas_call | solution.py:402
  (1 shorter events, 0.0 us)
Async XLA Ops:
  6.2 25.0 %all-to-all-start = ((f32[16,70,256]{2,1,0:T(8,128)}), f32[16,70,256]{2,1,0:T(8,128)S(1)}, u32[]{:S(2)}, u32[]{:S(2)}) async-start(f32[16,70,256]{2,1,0:T(8,128)} %drive.1), calls=%async_computation | async-start | bytes 2359296 | tf_op jit(solution)/shard_map/all_to_all | solution.py:376
  13.8 17.4 %copy-start = (f32[16,2,256]{2,1,0:T(2,128)S(1)}, f32[16,2,256]{2,1,0:T(2,128)}, u32[]{:S(2)}) copy-start(f32[16,2,256]{2,1,0:T(2,128)} %out_ref.1) | copy-start | bytes 98308

commit v7 on v6

--- a/solution.py
+++ b/solution.py
@@ -254,7 +254,7 @@
         odd = [out[k : k + 1] * kept[t] for k in range(2) for t in range(1, span, 2)]
         weights = jnp.concatenate(even + [blank] + odd + [blank], 0)
         flow = dot3(weights, state, NT)
-        back_ref[chunk] = jnp.concatenate([flow[:8], flow[8:]], 1)
+        back_ref[chunk] = jnp.concatenate([flow[:8], flow[8:]], 1)[:span]
         if chunk < chunks - 1:
             state = recv_ref[chunk, 0:scen] + product * state
 
@@ -385,7 +385,7 @@
         owner_kernel,
         in_specs=[WHOLE, WHOLE],
         out_specs=WHOLE,
-        out_shape=pltpu.VMEM((chunks, 8, lanes), F32),
+        out_shape=pltpu.VMEM((chunks, span, lanes), F32),
         compiler_params=pltpu.CompilerParams(vmem_limit_bytes=16 * 1024 * 1024),
         name="owner",
     )(owned, out_map)

time: 68.8 us -> 68.8 us (level)
  no operation moved by 1% of the time
where the time goes in v7:
time: 68.8 us; the launch traced here: 68.5 us
  blocking collectives  35.6 us (52%)
  Pallas kernels  15.9 us (23%)
  waiting for transfers between devices  9.33 us (14%)
  starting transfers between devices  7.59 us (11%)
    all_gather x1, blocking collectives, per_device(): every = lax.all_gather(joined, 'feeder', axis=0, tiled=False)  24.3 us
    all_to_all x1, blocking collectives, per_device(): back = lax.all_to_all(back, 'tm', 0, 0, tiled=True)  11.3 us
    all_to_all x1, waiting for transfers between devices, per_device(): owned = lax.all_to_all(send, 'tm', 0, 0, tiled=True)  9.33 us
    pallas_call x1, Pallas kernels, side_call(): pl.pallas_call(side_kernel, in_specs=[ANYWHERE] * 5 + [WHOLE] * 3 + [ANYW...  8.04 us
    all_to_all x1, starting transfers between devices, per_device(): owned = lax.all_to_all(send, 'tm', 0, 0, tiled=True)  7.59 us
    pallas_call x1, Pallas kernels, drive_call(): pl.pallas_call(drive_kernel, in_specs=[ANYWHERE] * 4, out_specs=ANYWHERE,...  6.19 us
  transfers between devices with their start and end apart: 1, of which 1 were waited for; matrix products, arithmetic and copies ran while one was open for 0% of the time, Pallas kernels for 12%

profile of v7, /device:TPU:1, one launch (start us, length us, event | category | flops | bytes accessed | tf_op | source)
XLA Modules:
  0.0 68.5 jit_solution(11114771934636404448)
XLA Ops:
  0.0 6.2 %drive.1 = f32[16,70,256]{2,1,0:T(8,128)} custom-call(s32[16]{0:T(128)} %counts_hbm.3, bf16[16,6,64,512]{3,2,1,0:T(8,128)(2,1)} %bitcast.10, bf16[16,512,256]{2,1,0:T(8,128)(2,1)} %map_hbm.3, f32[6,16,256]{2,1,0:T(8,128)} %bitcast.12), custom_call_target="tpu_custom_call" | custom-call | tf_op jit(solution)/shard_map/drive/pallas_call | solution.py:315
  6.2 7.6 %all-to-all-start = ((f32[16,70,256]{2,1,0:T(8,128)}), f32[16,70,256]{2,1,0:T(8,128)S(1)}, u32[]{:S(2)}, u32[]{:S(2)}) async-start(f32[16,70,256]{2,1,0:T(8,128)} %drive.1), calls=%async_computation | async-start | bytes 2359296 | tf_op jit(solution)/shard_map/all_to_all | solution.py:376
  13.8 0.0 copy-start
  13.8 8.0 %side.1 = (f32[7,16,128]{2,1,0:T(8,128)S(1)}, f32[6,16,256]{2,1,0:T(8,128)S(1)}) custom-call(s32[16]{0:T(128)} %counts_hbm.3, bf16[16,6,64,512]{3,2,1,0:T(8,128)(2,1)} %bitcast.11, bf16[16,512,256]{2,1,0:T(8,128)(2,1)} %map_hbm.3, f32[6,16,256]{2,1,0:T(8,128)} %bitcast.13, f32[16,2,256]{2,1,0:T(2,128)} %out_ref.1, s32[1,256]{1,0:T(1,128)} %bitcast.16, ...), custom_call_target="tpu_custom_call" | custom-call | flops 1610612736 | bytes 20971520 | tf_op jit(solution)/shard_map/side/pallas_call | solution.py:342
  21.9 9.3 %all-to-all-done.recv_ref = f32[16,70,256]{2,1,0:T(8,128)S(1)} async-done(((f32[16,70,256]{2,1,0:T(8,128)}), f32[16,70,256]{2,1,0:T(8,128)S(1)}, u32[]{:S(2)}, u32[]{:S(2)}) %all-to-all-start) | async-done | bytes 1146912 | tf_op jit(solution)/shard_map/all_to_all | solution.py:376
  31.2 0.0 copy-done
  31.2 0.5 owner.1
  31.7 11.3 %all_to_all.10.back_ref = f32[16,6,128]{2,1,0:T(8,128)S(1)} all-to-all(f32[16,6,128]{2,1,0:T(8,128)S(1)} %owner.1), channel_id=1, replica_groups=mesh['feeder'=16,'tm'=16] {'tm'}, dimensions={0} | all-to-all | bytes 98304 | tf_op jit(solution)/shard_map/all_to_all | solution.py:392
  43.1 24.3 %all-gather = f32[112,16,128]{2,1,0:T(8,128)S(1)} all-gather(f32[7,16,128]{2,1,0:T(8,128)S(1)} %join.1), channel_id=2, replica_groups=mesh['feeder'=16,'tm'=16] {'feeder'}, dimensions={0}, use_global_device_ids=true | all-gather | bytes 974848 | tf_op jit(solution)/shard_map/all_gather | solution.py:401
  67.3 1.2 %mix.1 = f32[6,16,64]{2,1,0:T(8,128)} custom-call(f32[6,16,256]{2,1,0:T(8,128)S(1)} %get-tuple-element.12.table_ref, f32[16,7,16,128]{3,2,1,0:T(8,128)S(1)} %bitcast.9), custom_call_target="tpu_custom_call" | custom-call | tf_op jit(solution)/shard_map/mix/pallas_call | solution.py:402
  (1 shorter events, 0.0 us)
Async XLA Ops:
  6.2 25.0 %all-to-all-start = ((f32[16,70,256]{2,1,0:T(8,128)}), f32[16,70,256]{2,1,0:T(8,128)S(1)}, u32[]{:S(2)}, u32[]{:S(2)}) async-start(f32[16,70,256]{2,1,0:T(8,128)} %drive.1), calls=%async_computation | async-start | bytes 2359296 | tf_op jit(solution)/shard_map/all_to_all | solution.py:376
  13.8 17.4 %copy-start = (f32[16,2,256]{2,1,0:T(2,128)S(1)}, f32[16,2,256]{2,1,0:T(2,128)}, u32[]{:S(2)}) copy-start(f32[16,2,256]{2,1,0:T(2,128)} %out_ref.1) | copy-start | bytes 98308
